TPU v7x, 32 devices: a whole 2x2x4 slice. The times are simulated.
32 devices in a mesh: dp: 2 (over y), ctx: 16 (over z, x, core).
Axes of the slice: x: 2, y: 2, z: 4, core: 2. Of those that a mesh axis runs over, the one named last changes fastest.
Arguments:
- positions: int32 [2, 768], P('dp', 'ctx'), may hold values from -1 to 2047, as said below
- queries: bfloat16 [2, 768, 3072], P('dp', 'ctx'), may hold values from -6 to 6
- keys: bfloat16 [2, 768, 512], P('dp', 'ctx'), may hold values from -6 to 6
- values: bfloat16 [2, 768, 512], P('dp', 'ctx'), may hold values from -6 to 6
- router_logits: float32 [2, 768], P('dp', 'ctx'), may hold values from -6 to 6
- out_cotangent: bfloat16 [2, 768, 3072], P('dp', 'ctx'), may hold values from -24 to 24
- query_gain: float32 [128], replicated, may hold values from 0.8 to 5.5
- key_gain: float32 [128], replicated, may hold values from 0.8 to 5.5
Outputs:
- block_out: bfloat16 [2, 768, 3072], P('dp', 'ctx')
- grad_queries: bfloat16 [2, 768, 3072], P('dp', 'ctx')
- grad_keys: bfloat16 [2, 768, 512], P('dp', 'ctx')
- grad_values: bfloat16 [2, 768, 512], P('dp', 'ctx')
- grad_logits: float32 [2, 768], P('dp', 'ctx')
- grad_query_gain: float32 [128], replicated
- grad_key_gain: float32 [128], replicated
Inputs may be any that keep to these rules, and one draw needn't show every extreme that they name: For each sequence and each device along ctx, the device's 48 slots hold, in rising order, the positions of the device's selected tokens, all within the device's own block of 128 positions, followed by -1 in the slots it leaves unused. Every aligned run of 4 devices selects exactly 64 tokens; a device selects at most 48 tokens, and in every sequence some device selects exactly 48. The last device of every sequence selects position 2047.
All inputs are finite; a program needn't handle non-finite values.
Results may differ from a plain program's by a relative error of at most 0.023.
The roundings to bfloat16 on the way count: a program that leaves them out, or rounds other values in their place, can miss the bound.
Values may be sent and summed in bfloat16 or wider, within the bound.
A program may use at most 64 MiB of HBM per device.

v0:
```python
import math

import jax
import jax.numpy as jnp
from jax import lax
from jax.sharding import PartitionSpec as P

SEL_DEV = 16


rope_base = 1000000.0
norm_eps = 1e-06


def entering(part, axis, combine, identity):
    place = lax.axis_index(axis)
    gathered = lax.all_gather(part, axis)
    state = jnp.zeros_like(part) + jnp.asarray(identity, part.dtype)

    def one(step, state):
        return combine(state, lax.dynamic_index_in_dim(gathered, step, 0, False))

    return lax.fori_loop(0, place, one, state)


def shifted(value, axis, by):
    peers = lax.axis_size(axis)
    pairs = [(i, i + by) for i in range(peers) if 0 <= i + by < peers]
    return lax.ppermute(value, axis, pairs)


def rope_tables(token_pos, head_size):
    index_row = jnp.arange(head_size // 2).astype(jnp.float32)
    frequency = jnp.exp(index_row * (-2.0 * math.log(rope_base) / head_size))
    angles = token_pos.astype(jnp.float32)[:, None] * frequency[None, :]
    return (jnp.cos(angles)[:, None, :], jnp.sin(angles)[:, None, :])


def rotate(source, cos_table, sine_table, direction):
    half_size = source.shape[-1] // 2
    lead_half = source[..., :half_size]
    tail_half = source[..., half_size:]
    return jnp.concatenate(
        [
            lead_half * cos_table - direction * tail_half * sine_table,
            direction * lead_half * sine_table + tail_half * cos_table,
        ],
        axis=-1,
    )


def normalize(source, gain_vec, cos_table, sine_table, head_total):
    heads_view = source.astype(jnp.float32).reshape(source.shape[0], head_total, -1)
    inv_rms = lax.rsqrt(jnp.mean(heads_view * heads_view, axis=-1, keepdims=True) + norm_eps)
    unit_rows = heads_view * inv_rms
    return (rotate(unit_rows * gain_vec, cos_table, sine_table, 1.0), unit_rows, inv_rms)


def norm_grad(grad_rot, unit_rows, inv_rms, gain_vec, cos_table, sine_table):
    unrotated = rotate(grad_rot.astype(jnp.float32), cos_table, sine_table, -1.0)
    gain_term = jnp.sum(unrotated * unit_rows, axis=(0, 1))
    scaled = unrotated * gain_vec
    grad_input = inv_rms * (
        scaled - unit_rows * jnp.mean(scaled * unit_rows, axis=-1, keepdims=True)
    )
    return (grad_input, gain_term)


def add_counts(earlier, later):
    return earlier + later


def routing(owners, slot_in_owner, live_mask, my_index, max_shift, per_owner):
    shift_range = jnp.arange(-max_shift, max_shift + 1, dtype=jnp.int32)
    targets = my_index + shift_range
    slot_ids = jnp.arange(per_owner, dtype=jnp.int32)
    matches = (
        live_mask[None, None, :]
        & (owners[None, None, :] == targets[:, None, None])
        & (slot_in_owner[None, None, :] == slot_ids[None, :, None])
    )
    return matches.astype(jnp.bfloat16)


def deliver(payload, routes, max_shift, mover):
    outgoing = jnp.einsum(
        "osc,cw->osw", routes, payload, preferred_element_type=jnp.float32
    ).astype(jnp.bfloat16)
    arrived = outgoing[max_shift]
    for offset in range(-max_shift, max_shift + 1):
        if offset != 0:
            arrived = arrived + mover(outgoing[offset + max_shift], offset)
    return arrived


def collect(results, routes, max_shift, mover):
    pieces = [
        results if offset == 0 else mover(results, -offset)
        for offset in range(-max_shift, max_shift + 1)
    ]
    return jnp.einsum(
        "osc,osw->cw", routes, jnp.stack(pieces), preferred_element_type=jnp.float32
    ).astype(jnp.bfloat16)


def attend(query_rows, cotan_rows, query_rank, keys_all, heads_k, head_size):
    row_count = query_rows.shape[0]
    key_count = keys_all.shape[0]
    width_k = heads_k * head_size
    group_size = query_rows.shape[1] // width_k
    score_scale = 1.0 / math.sqrt(head_size)
    query_grouped = query_rows.reshape(row_count, heads_k, group_size, head_size)
    cotan_grouped = cotan_rows.reshape(row_count, heads_k, group_size, head_size)
    key_heads = keys_all[:, :width_k].reshape(key_count, heads_k, head_size)
    value_heads = keys_all[:, width_k:].reshape(key_count, heads_k, head_size)
    allowed = jnp.arange(key_count, dtype=jnp.int32)[None, :] <= query_rank[:, None]
    scores = (
        jnp.einsum("rgqd,kgd->gqrk", query_grouped, key_heads, preferred_element_type=jnp.float32)
        * score_scale
    )
    scores = jnp.where(allowed[None, None], scores, -jnp.inf)
    row_max = jnp.max(scores, axis=-1, keepdims=True)
    exp_scores = jnp.exp(scores - row_max)
    probs = exp_scores / jnp.sum(exp_scores, axis=-1, keepdims=True)
    prob_round = probs.astype(jnp.bfloat16)
    attended = jnp.einsum(
        "gqrk,kgd->rgqd", prob_round, value_heads, preferred_element_type=jnp.float32
    ).astype(jnp.bfloat16)
    row_delta = jnp.einsum(
        "rgqd,rgqd->gqr", cotan_grouped, attended, preferred_element_type=jnp.float32
    )
    grad_prob = jnp.einsum(
        "rgqd,kgd->gqrk", cotan_grouped, value_heads, preferred_element_type=jnp.float32
    )
    dscore = (probs * (grad_prob - row_delta[..., None])).astype(jnp.bfloat16)
    grad_rows = (
        jnp.einsum("gqrk,kgd->rgqd", dscore, key_heads, preferred_element_type=jnp.float32)
        * score_scale
    ).astype(jnp.bfloat16)

    def key_term(start, count):
        grad_keys = (
            jnp.einsum("gqrk,rgqd->kgd", dscore, query_grouped, preferred_element_type=jnp.float32)
            * score_scale
        )
        grad_vals = jnp.einsum(
            "gqrk,rgqd->kgd", prob_round, cotan_grouped, preferred_element_type=jnp.float32
        )
        return jnp.concatenate(
            [grad_keys.reshape(count, width_k), grad_vals.reshape(count, width_k)], axis=1
        )

    return (attended.reshape(row_count, -1), grad_rows.reshape(row_count, -1), key_term)


def per_device(
    positions, queries, keys, values, router_logits, out_cotangent, query_gain, key_gain
):
    token_pos = positions[0]
    capacity = token_pos.shape[0]
    head_size = query_gain.shape[0]
    width_q = queries.shape[2]
    width_k = keys.shape[2]
    heads_q = width_q // head_size
    heads_k = width_k // head_size
    per_owner = SEL_DEV
    max_shift = capacity // per_owner - 1
    live_mask = token_pos >= 0
    counts_here = jnp.sum(live_mask.astype(jnp.int32))[None]
    my_index = lax.axis_index("ctx")
    offset_base = entering(counts_here, "ctx", add_counts, jnp.zeros((1,), jnp.int32))[0]
    ranking = offset_base + jnp.arange(capacity, dtype=jnp.int32)
    owners = ranking // per_owner
    slot_in_owner = ranking % per_owner
    routes = routing(owners, slot_in_owner, live_mask, my_index, max_shift, per_owner)
    cos_table, sine_table = rope_tables(token_pos, head_size)
    q_rot, q_unit, q_inv = normalize(queries[0], query_gain, cos_table, sine_table, heads_q)
    k_rot, k_unit, k_inv = normalize(keys[0], key_gain, cos_table, sine_table, heads_k)
    query_round = q_rot.reshape(capacity, width_q).astype(jnp.bfloat16)
    key_round = k_rot.reshape(capacity, width_k).astype(jnp.bfloat16)
    gating = jax.nn.sigmoid(router_logits[0])
    live_rows = live_mask.astype(jnp.float32)
    cotan_round = ((gating * live_rows)[:, None] * out_cotangent[0].astype(jnp.float32)).astype(
        jnp.bfloat16
    )
    kv_local = jnp.concatenate([key_round, values[0]], axis=1)
    arrived = deliver(
        jnp.concatenate([query_round, cotan_round, kv_local], axis=1),
        routes,
        max_shift,
        lambda message, offset: shifted(message, "ctx", offset),
    )
    query_rows = arrived[:, :width_q]
    cotan_rows = arrived[:, width_q : 2 * width_q]
    kv_rows = arrived[:, 2 * width_q :]
    query_rank = my_index * per_owner + jnp.arange(per_owner, dtype=jnp.int32)
    keys_all = lax.all_gather(kv_rows, "ctx", axis=0, tiled=True)
    attended_rows, grad_rows, key_term = attend(
        query_rows, cotan_rows, query_rank, keys_all, heads_k, head_size
    )
    kv_grad = lax.psum_scatter(
        key_term(jnp.int32(0), per_owner * lax.axis_size("ctx")),
        "ctx",
        scatter_dimension=0,
        tiled=True,
    ).astype(jnp.bfloat16)
    returned = collect(
        jnp.concatenate([attended_rows, grad_rows, kv_grad], axis=1),
        routes,
        max_shift,
        lambda message, offset: shifted(message, "ctx", offset),
    )
    attended_home = returned[:, :width_q]
    grad_home = returned[:, width_q : 2 * width_q]
    kv_back = returned[:, 2 * width_q :]
    attended_f = attended_home.astype(jnp.float32)
    block_out = ((gating * live_rows)[:, None] * attended_f).astype(jnp.bfloat16)
    grad_logits = (1.0 - gating) * jnp.sum(cotan_round.astype(jnp.float32) * attended_f, axis=-1)
    query_grad, query_term = norm_grad(
        grad_home.reshape(capacity, heads_q, head_size),
        q_unit,
        q_inv,
        query_gain,
        cos_table,
        sine_table,
    )
    key_grad, key_term_sum = norm_grad(
        kv_back[:, :width_k].reshape(capacity, heads_k, head_size),
        k_unit,
        k_inv,
        key_gain,
        cos_table,
        sine_table,
    )
    grad_values = kv_back[:, width_k:]
    gain_sums = lax.psum((query_term, key_term_sum), ("dp", "ctx"))
    selected_all = lax.axis_size("dp") * lax.axis_size("ctx") * per_owner
    grad_query_gain = gain_sums[0] / math.sqrt(selected_all * heads_q)
    grad_key_gain = gain_sums[1] / math.sqrt(selected_all * heads_k)
    grad_queries = (query_grad.reshape(capacity, width_q) * live_rows[:, None]).astype(jnp.bfloat16)
    grad_keys = (key_grad.reshape(capacity, width_k) * live_rows[:, None]).astype(jnp.bfloat16)
    return (
        block_out[None],
        grad_queries[None],
        grad_keys[None],
        grad_values[None],
        grad_logits[None],
        grad_query_gain,
        grad_key_gain,
    )


def solution(mesh):
    return jax.shard_map(
        per_device,
        mesh=mesh,
        in_specs=(
            P("dp", "ctx"),
            P("dp", "ctx", None),
            P("dp", "ctx", None),
            P("dp", "ctx", None),
            P("dp", "ctx"),
            P("dp", "ctx", None),
            P(),
            P(),
        ),
        out_specs=(
            P("dp", "ctx", None),
            P("dp", "ctx", None),
            P("dp", "ctx", None),
            P("dp", "ctx", None),
            P("dp", "ctx"),
            P(),
            P(),
        ),
        check_vma=False,
    )
```

profile of v0, /device:TPU:0, one launch (start us, length us, event | category | flops | bytes accessed | tf_op | source)
XLA Modules:
  0.0 223.1 jit_solution(743004364612513797)
XLA Ops:
  7.9 1.3 convert_reduce_fusion
  9.2 1.1 fusion.54
  15.0 1.4 dynamic-update-slice
  16.4 13.7 %all-reduce = s32[16]{0:T(128)S(1)} all-reduce(s32[16]{0:T(128)S(1)} %dynamic-update-slice), channel_id=1, replica_groups=mesh['dp'=2,'ctx'=16] {'ctx'}, use_global_device_ids=true, to_apply=%add | all-reduce | flops 16 | bytes 128
  32.0 1.3 collective-permute-start
  33.3 1.3 collective-permute-start.1
  34.6 3.7 %collective-permute-start.2 = (bf16[16,7168]{1,0:T(8,128)(2,1)S(1)}, bf16[16,7168]{1,0:T(8,128)(2,1)}, u32[]{:S(2)}, u32[]{:S(2)}) collective-permute-start(bf16[16,7168]{1,0:T(8,128)(2,1)S(1)} %get-tuple-element.51), channel_id=1, source_target_pairs={{0,1},{1,2},{2,3},{3,4},{4,5},{5,6},{6,7},{7,8},{8,9},{9,10},{10,1... | collective-permute-start | bytes 688136 | tf_op jit(solution)/shard_map/ppermute | solution.py:29
  38.4 5.9 %collective-permute-start.3 = (bf16[16,7168]{1,0:T(8,128)(2,1)S(1)}, bf16[16,7168]{1,0:T(8,128)(2,1)}, u32[]{:S(2)}, u32[]{:S(2)}) collective-permute-start(bf16[16,7168]{1,0:T(8,128)(2,1)S(1)} %get-tuple-element.50), channel_id=1, source_target_pairs={{0,2},{1,3},{2,4},{3,5},{4,6},{5,7},{6,8},{7,9},{8,10},{9,11},{10,... | collective-permute-start | bytes 688136 | tf_op jit(solution)/shard_map/ppermute | solution.py:29
  44.4 6.2 %collective-permute-done.3 = bf16[16,7168]{1,0:T(8,128)(2,1)} collective-permute-done((bf16[16,7168]{1,0:T(8,128)(2,1)S(1)}, bf16[16,7168]{1,0:T(8,128)(2,1)}, u32[]{:S(2)}, u32[]{:S(2)}) %collective-permute-start.3) | collective-permute-done | bytes 229408 | tf_op jit(solution)/shard_map/ppermute | solution.py:29
  50.6 1.3 fusion.29
  51.9 34.6 %all_gather.7 = bf16[256,1024]{1,0:T(8,128)(2,1)S(1)} all-gather(bf16[16,1024]{1,0:T(8,128)(2,1)S(1)} %slice.100), channel_id=1, replica_groups=mesh['dp'=2,'ctx'=16] {'ctx'}, dimensions={0}, use_global_device_ids=true | all-gather | bytes 557056 | tf_op jit(solution)/shard_map/all_gather | solution.py:197
  87.0 1.1 fusion.75
  88.1 0.9 fusion.31
  89.9 1.2 fusion.9
  92.2 1.1 pad_maximum_fusion
  93.9 54.3 %reduce-scatter.2.cloned.1.call-done = f32[16,1024]{1,0:T(8,128)} async-done(((f32[256,1024]{1,0:T(8,128)}), f32[16,1024]{1,0:T(8,128)}) %reduce-scatter.2.cloned.1.call-update) | async-done | bytes 65552 | tf_op jit(solution)/shard_map/reduce_scatter | solution.py:201
  149.0 3.2 %collective-permute-start.4 = (bf16[16,7168]{1,0:T(8,128)(2,1)S(1)}, bf16[16,7168]{1,0:T(8,128)(2,1)S(1)}, u32[]{:S(2)}, u32[]{:S(2)}) collective-permute-start(bf16[16,7168]{1,0:T(8,128)(2,1)S(1)} %pad_maximum_fusion.3), channel_id=1, source_target_pairs={{0,2},{1,3},{2,4},{3,5},{4,6},{5,7},{6,8},{7,9},{8,10},{9,11},{10,... | collective-permute-start | bytes 688136 | tf_op jit(solution)/shard_map/ppermute | solution.py:29
  152.7 1.3 collective-permute-start.5
  154.1 1.3 collective-permute-start.6
  155.4 1.3 collective-permute-start.7
  156.7 2.5 %collective-permute-done.6 = bf16[16,7168]{1,0:T(8,128)(2,1)S(1)} collective-permute-done((bf16[16,7168]{1,0:T(8,128)(2,1)S(1)}, bf16[16,7168]{1,0:T(8,128)(2,1)S(1)}, u32[]{:S(2)}, u32[]{:S(2)}) %collective-permute-start.6) | collective-permute-done | bytes 229408 | tf_op jit(solution)/shard_map/ppermute | solution.py:29
  159.2 9.5 %collective-permute-done.7 = bf16[16,7168]{1,0:T(8,128)(2,1)S(1)} collective-permute-done((bf16[16,7168]{1,0:T(8,128)(2,1)S(1)}, bf16[16,7168]{1,0:T(8,128)(2,1)S(1)}, u32[]{:S(2)}, u32[]{:S(2)}) %collective-permute-start.7) | collective-permute-done | bytes 229408 | tf_op jit(solution)/shard_map/ppermute | solution.py:29
  169.9 1.0 fusion.19
  174.6 40.2 %all-reduce.1 = (f32[128]{0:T(128)S(1)}, f32[128]{0:T(128)S(1)}) all-reduce(f32[128]{0:T(128)S(1)} %bitcast_reduce_fusion, f32[128]{0:T(128)S(1)} %bitcast_reduce_fusion.1), channel_id=1, replica_groups=mesh['dp'=2,'ctx'=16] {'dp','ctx'}, use_global_device_ids=true, to_apply=%region_13.14 | all-reduce | flops 256 | bytes 2048 | tf_op jit(solution)/shard_map/psum | solution.py:236
  (118 shorter events, 17.8 us)
Async XLA Ops:
  7.2 5.4 %copy-start = (bf16[1,48,3072]{2,1,0:T(8,128)(2,1)S(1)}, bf16[1,48,3072]{2,1,0:T(8,128)(2,1)}, u32[]{:S(2)}) copy-start(bf16[1,48,3072]{2,1,0:T(8,128)(2,1)} %param.11) | copy-start | bytes 884740
  7.2 141.0 %reduce-scatter.2.cloned.1.call-start = ((), (), s32[]{:S(2)}) async-start(), calls=%async_computation.1 | async-start | bytes 1114112 | tf_op jit(solution)/shard_map/reduce_scatter | solution.py:201
  12.6 0.7 copy-start.6
  13.7 0.7 copy-start.12
  13.7 16.4 %copy-start.8 = (s32[1,48]{1,0:T(1,128)S(1)}, s32[1,48]{1,0:T(1,128)}, u32[]{:S(2)}) copy-start(s32[1,48]{1,0:T(1,128)} %param.10) | copy-start | bytes 580
  13.7 16.4 %copy-start.9 = (f32[1,48]{1,0:T(1,128)S(1)}, f32[1,48]{1,0:T(1,128)}, u32[]{:S(2)}) copy-start(f32[1,48]{1,0:T(1,128)} %param.14) | copy-start | bytes 580
  13.8 16.9 %copy-start.1 = (bf16[1,48,3072]{2,1,0:T(8,128)(2,1)S(1)}, bf16[1,48,3072]{2,1,0:T(8,128)(2,1)}, u32[]{:S(2)}) copy-start(bf16[1,48,3072]{2,1,0:T(8,128)(2,1)} %param.15) | copy-start | bytes 884740
  13.8 17.1 %copy-start.11 = (bf16[1,48,512]{2,1,0:T(8,128)(2,1)S(1)}, bf16[1,48,512]{2,1,0:T(8,128)(2,1)}, u32[]{:S(2)}) copy-start(bf16[1,48,512]{2,1,0:T(8,128)(2,1)} %param.13) | copy-start | bytes 147460
  32.0 12.3 %collective-permute-start = (bf16[16,7168]{1,0:T(8,128)(2,1)}, bf16[16,7168]{1,0:T(8,128)(2,1)}, u32[]{:S(2)}, u32[]{:S(2)}) collective-permute-start(bf16[16,7168]{1,0:T(8,128)(2,1)} %get-tuple-element.49), channel_id=1, source_target_pairs={{2,0},{3,1},{4,2},{5,3},{6,4},{7,5},{8,6},{9,7},{10,8},{11,9},{12,... | collective-permute-start | bytes 688136 | tf_op jit(solution)/shard_map/ppermute | solution.py:29
  33.3 11.0 %collective-permute-start.1 = (bf16[16,7168]{1,0:T(8,128)(2,1)S(1)}, bf16[16,7168]{1,0:T(8,128)(2,1)}, u32[]{:S(2)}, u32[]{:S(2)}) collective-permute-start(bf16[16,7168]{1,0:T(8,128)(2,1)S(1)} %get-tuple-element.52), channel_id=1, source_target_pairs={{1,0},{2,1},{3,2},{4,3},{5,4},{6,5},{7,6},{8,7},{9,8},{10,9},{11,1... | collective-permute-start | bytes 688136 | tf_op jit(solution)/shard_map/ppermute | solution.py:29
  34.6 9.8 %collective-permute-start.2 = (bf16[16,7168]{1,0:T(8,128)(2,1)S(1)}, bf16[16,7168]{1,0:T(8,128)(2,1)}, u32[]{:S(2)}, u32[]{:S(2)}) collective-permute-start(bf16[16,7168]{1,0:T(8,128)(2,1)S(1)} %get-tuple-element.51), channel_id=1, source_target_pairs={{0,1},{1,2},{2,3},{3,4},{4,5},{5,6},{6,7},{7,8},{8,9},{9,10},{10,1... | collective-permute-start | bytes 688136 | tf_op jit(solution)/shard_map/ppermute | solution.py:29
  38.4 12.2 %collective-permute-start.3 = (bf16[16,7168]{1,0:T(8,128)(2,1)S(1)}, bf16[16,7168]{1,0:T(8,128)(2,1)}, u32[]{:S(2)}, u32[]{:S(2)}) collective-permute-start(bf16[16,7168]{1,0:T(8,128)(2,1)S(1)} %get-tuple-element.50), channel_id=1, source_target_pairs={{0,2},{1,3},{2,4},{3,5},{4,6},{5,7},{6,8},{7,9},{8,10},{9,11},{10,... | collective-permute-start | bytes 688136 | tf_op jit(solution)/shard_map/ppermute | solution.py:29
  91.1 0.7 copy-start.3
  92.2 1.1 copy-start.4
  93.3 58.9 %copy-start.5 = (f32[128]{0:T(128)S(1)}, f32[128]{0:T(128)}, u32[]{:S(2)}) copy-start(f32[128]{0:T(128)} %param.17) | copy-start | bytes 1540
  149.0 7.6 %collective-permute-start.4 = (bf16[16,7168]{1,0:T(8,128)(2,1)S(1)}, bf16[16,7168]{1,0:T(8,128)(2,1)S(1)}, u32[]{:S(2)}, u32[]{:S(2)}) collective-permute-start(bf16[16,7168]{1,0:T(8,128)(2,1)S(1)} %pad_maximum_fusion.3), channel_id=1, source_target_pairs={{0,2},{1,3},{2,4},{3,5},{4,6},{5,7},{6,8},{7,9},{8,10},{9,11},{10,... | collective-permute-start | bytes 688136 | tf_op jit(solution)/shard_map/ppermute | solution.py:29
  152.7 3.9 %collective-permute-start.5 = (bf16[16,7168]{1,0:T(8,128)(2,1)S(1)}, bf16[16,7168]{1,0:T(8,128)(2,1)S(1)}, u32[]{:S(2)}, u32[]{:S(2)}) collective-permute-start(bf16[16,7168]{1,0:T(8,128)(2,1)S(1)} %pad_maximum_fusion.3), channel_id=1, source_target_pairs={{0,1},{1,2},{2,3},{3,4},{4,5},{5,6},{6,7},{7,8},{8,9},{9,10},{10,1... | collective-permute-start | bytes 688136 | tf_op jit(solution)/shard_map/ppermute | solution.py:29
  154.1 5.2 %collective-permute-start.6 = (bf16[16,7168]{1,0:T(8,128)(2,1)S(1)}, bf16[16,7168]{1,0:T(8,128)(2,1)S(1)}, u32[]{:S(2)}, u32[]{:S(2)}) collective-permute-start(bf16[16,7168]{1,0:T(8,128)(2,1)S(1)} %pad_maximum_fusion.3), channel_id=1, source_target_pairs={{1,0},{2,1},{3,2},{4,3},{5,4},{6,5},{7,6},{8,7},{9,8},{10,9},{11,1... | collective-permute-start | bytes 688136 | tf_op jit(solution)/shard_map/ppermute | solution.py:29
  155.4 13.4 %collective-permute-start.7 = (bf16[16,7168]{1,0:T(8,128)(2,1)S(1)}, bf16[16,7168]{1,0:T(8,128)(2,1)S(1)}, u32[]{:S(2)}, u32[]{:S(2)}) collective-permute-start(bf16[16,7168]{1,0:T(8,128)(2,1)S(1)} %pad_maximum_fusion.3), channel_id=1, source_target_pairs={{2,0},{3,1},{4,2},{5,3},{6,4},{7,5},{8,6},{9,7},{10,8},{11,9},{12,... | collective-permute-start | bytes 688136 | tf_op jit(solution)/shard_map/ppermute | solution.py:29
  169.8 1.7 copy-start.2
  169.9 1.7 copy-start.7
  173.6 42.1 %copy-start.10 = (f32[1,48]{1,0:T(1,128)S(1)}, f32[1,48]{1,0:T(1,128)}, u32[]{:S(2)}) copy-start(f32[1,48]{1,0:T(1,128)} %get-tuple-element.46) | copy-start | bytes 580
Sparse Core Ops, SparseCore 0:
  93.5 54.6 reduce-scatter.1
where the time goes:
time: 224 us; the launch traced here: 223 us
  blocking collectives  88.4 us (39%)
  waiting for transfers between devices  72.4 us (32%)
  starting transfers between devices  19.3 us (9%)
  other arithmetic  15.6 us (7%)
  between operations  14.7 us (7%)
  local copies, waits for them, and re-layouts  7.23 us (3%)
  matrix products  5.42 us (2%)
    reduce_scatter x1, waiting for transfers between devices, per_device(): lax.psum_scatter(key_term(jnp.int32(0), per_owner * lax.axis_size('ctx'))...  54.3 us
    psum x1, blocking collectives, per_device(): gain_sums = lax.psum((query_term, key_term_sum), ('dp', 'ctx'))  40.2 us
    all_gather x1, blocking collectives, per_device(): keys_all = lax.all_gather(kv_rows, 'ctx', axis=0, tiled=True)  34.6 us
    ppermute x8, starting transfers between devices, shifted(): return lax.ppermute(value, axis, pairs)  19.3 us
    ppermute x8, waiting for transfers between devices, shifted(): return lax.ppermute(value, axis, pairs)  18.2 us
    unnamed x1, blocking collectives  13.7 us
  transfers between devices with their start and end apart: 9, of which 4 were waited for; matrix products, arithmetic and copies ran while one was open for 1% of the time, Pallas kernels for 0%

commit v1 on v0

v1 whole, which is shorter than its diff:
```python
import functools
import math

import jax
import jax.numpy as jnp
from jax import lax
from jax.experimental import pallas as pl
from jax.experimental.pallas import tpu as pltpu
from jax.sharding import PartitionSpec as P

SEL_DEV = 16
SEG_DEV = 4

rope_base = 1000000.0
norm_eps = 1e-06

F32 = jnp.float32
BF16 = jnp.bfloat16


def dot(a, b, dims):
    return lax.dot_general(a, b, (dims, ((), ())), preferred_element_type=F32)


NN = ((1,), (0,))
NT = ((1,), (1,))
TN = ((0,), (0,))


def kernel(
    n_seg,
    n_dp,
    aux_ref,
    q_ref,
    k_ref,
    v_ref,
    c_ref,
    gain_ref,
    out_ref,
    gq_ref,
    gk_ref,
    gv_ref,
    gl_ref,
    gains_ref,
    skv,
    rkv,
    sqd,
    rqd,
    qunit,
    qinv,
    dround,
    kunit,
    kinv,
    kv_all,
    dkv_p,
    dkv_r,
    sback,
    rback,
    skb,
    rkb,
    gplane,
    gseg,
    gdp,
    kv_s,
    kv_r,
    qd_s,
    qd_r,
    z_s,
    z_r,
    dz_s,
    dz_r,
    b_s,
    b_r,
    kb_s,
    kb_r,
    g_s,
    g_r,
):
    cap, width_q = q_ref.shape
    width_k = k_ref.shape[1]
    head = gain_ref.shape[1]
    heads_k = width_k // head
    group = width_q // width_k
    gw = group * head
    sel = SEL_DEV * SEG_DEV
    pad = rkv.shape[1]
    scale = 1.0 / math.sqrt(head)

    my_dp = lax.axis_index("dp")
    my_ctx = lax.axis_index("ctx")
    seg = my_ctx // SEG_DEV
    g = my_ctx % SEG_DEV
    mate = {0: g, 1: g + 1 - 2 * (g % 2), 2: (g + 2) % 4, 3: 3 - g}
    plane = {o: seg * SEG_DEV + mate[o] for o in (1, 2, 3)}
    far = {o: (seg + o) % n_seg for o in range(1, n_seg)}
    far_dev = {o: far[o] * SEG_DEV + g for o in far}
    rows_dp = {o: (my_dp + o) % n_dp for o in range(1, n_dp)}
    order = (2, 3, 1)

    def remote(src, dst, ssem, rsem, ctx=None, dp=None):
        return pltpu.make_async_remote_copy(
            src_ref=src,
            dst_ref=dst,
            send_sem=ssem,
            recv_sem=rsem,
            device_id=(my_dp if dp is None else dp, my_ctx if ctx is None else ctx),
            device_id_type=pl.DeviceIdType.MESH,
        )

    barrier = pltpu.get_barrier_semaphore()
    peers = [(my_dp, plane[o]) for o in order]
    peers += [(my_dp, far_dev[o]) for o in far]
    peers += [(rows_dp[o], my_ctx) for o in rows_dp]
    for peer in peers:
        pl.semaphore_signal(barrier, inc=1, device_id=peer, device_id_type=pl.DeviceIdType.MESH)

    cos = aux_ref[0]
    sin = aux_ref[1]
    gate = aux_ref[2]
    valid = aux_ref[3]
    gain_q = gain_ref[0:1]
    gain_k = gain_ref[1:2]

    def normed(x):
        inv = lax.rsqrt(jnp.mean(x * x, axis=-1, keepdims=True) + norm_eps)
        return x * inv, inv

    def rot(x, direction):
        turned = pltpu.roll(x, head // 2, axis=1) * sin
        return x * cos + turned if direction > 0 else x * cos - turned

    count = jnp.sum(valid, axis=0, keepdims=True)
    count = jnp.broadcast_to(jnp.concatenate([count, count], axis=1), (pad - cap, 2 * head))
    for t in range(heads_k):
        cols = pl.ds(t * head, head)
        unit, inv = normed(k_ref[:, cols].astype(F32))
        kunit[t] = unit
        kinv[t] = jnp.broadcast_to(inv, (cap, head))
        skv[t, 0:cap, 0:head] = rot(unit * gain_k, 1).astype(BF16)
        skv[t, 0:cap, head:] = v_ref[:, cols]
        skv[t, cap:, :] = count.astype(BF16)

    pl.semaphore_wait(barrier, len(peers))

    kv_copies = []
    for o in order:
        copy = remote(skv.at[mate[o]], rkv.at[g], kv_s.at[o], kv_r.at[o], ctx=plane[o])
        copy.start()
        kv_copies.append(copy)
    rkv[g] = skv[g]

    qd_copies = []
    for o in order + (0,):
        t = mate[o]
        for j in range(group):
            cols = pl.ds(pl.multiple_of(t * gw + j * head, head), head)
            unit, inv = normed(q_ref[:, cols].astype(F32))
            qunit[t * group + j] = unit
            qinv[t * group + j] = jnp.broadcast_to(inv, (cap, head))
            turned = rot(unit * gain_q, 1).astype(BF16)
            weighted = (gate * c_ref[:, cols].astype(F32)).astype(BF16)
            dround[t * group + j] = weighted
            if o == 0:
                rqd[g, 0:cap, j * head : (j + 1) * head] = turned
                rqd[g, 0:cap, gw + j * head : gw + (j + 1) * head] = weighted
            else:
                sqd[o - 1, :, j * head : (j + 1) * head] = turned
                sqd[o - 1, :, gw + j * head : gw + (j + 1) * head] = weighted
        if o != 0:
            copy = remote(
                sqd.at[o - 1], rqd.at[g, pl.ds(0, cap)], qd_s.at[o], qd_r.at[o], ctx=plane[o]
            )
            copy.start()
            qd_copies.append(copy)
    for m in range(SEG_DEV):
        rqd[m, cap:, :] = jnp.zeros((pad - cap, 2 * gw), BF16)

    for copy in kv_copies:
        copy.wait_recv()
    wide = SEG_DEV * pad
    lane = lax.broadcasted_iota(jnp.int32, (1, wide), 1)
    member = lane // pad
    slot = (lane % pad).astype(F32)
    counts = [rkv[m, cap : cap + 16, :].astype(F32)[0:1] for m in range(SEG_DEV)]
    have = counts[0]
    base = jnp.zeros_like(have)
    run = counts[0]
    for m in range(1, SEG_DEV):
        have = jnp.where(member == m, counts[m], have)
        base = jnp.where(member == m, run, base)
        run = run + counts[m]
    place = jnp.where(slot < have, base + slot, -1.0)
    rank = lax.broadcasted_iota(jnp.int32, (sel, wide), 0).astype(F32)
    pick = jnp.where(rank == place, 1.0, 0.0).astype(BF16)
    kv_all[seg] = dot(pick, rkv[...].reshape(wide, 2 * head), NN).astype(BF16)
    z_copies = []
    for o in far:
        copy = remote(kv_all.at[seg], kv_all.at[seg], z_s.at[o], z_r.at[o], ctx=far_dev[o])
        copy.start()
        z_copies.append(copy)

    for copy in qd_copies:
        copy.wait_recv()
    qd = dot(pick, rqd[...].reshape(wide, 2 * gw), NN).astype(BF16)
    q_rows = jnp.concatenate([qd[:, j * head : (j + 1) * head] for j in range(group)], axis=0)
    d_rows = jnp.concatenate(
        [qd[:, gw + j * head : gw + (j + 1) * head] for j in range(group)], axis=0
    )
    for copy in z_copies:
        copy.wait_recv()

    total = n_seg * sel
    keys = kv_all[:, :, 0:head].reshape(total, head)
    vals = kv_all[:, :, head:].reshape(total, head)
    row = lax.broadcasted_iota(jnp.int32, (group * sel, total), 0) % sel
    col = lax.broadcasted_iota(jnp.int32, (group * sel, total), 1)
    scores = dot(q_rows, keys, NT) * scale
    scores = jnp.where(col <= row + seg * sel, scores, -jnp.inf)
    top = jnp.max(scores, axis=-1, keepdims=True)
    exps = jnp.exp(scores - top)
    probs = exps / jnp.sum(exps, axis=-1, keepdims=True)
    probs_b = probs.astype(BF16)
    attended = dot(probs_b, vals, NN).astype(BF16)
    delta = jnp.sum(d_rows.astype(F32) * attended.astype(F32), axis=-1, keepdims=True)
    dprob = dot(d_rows, vals, NT)
    dscore = (probs * (dprob - delta)).astype(BF16)
    dkv_p[:, :, 0:head] = (dot(dscore, q_rows, TN) * scale).reshape(n_seg, sel, head)
    dkv_p[:, :, head:] = dot(probs_b, d_rows, TN).reshape(n_seg, sel, head)
    dz_copies = []
    for o in far:
        copy = remote(dkv_p.at[far[o]], dkv_r.at[seg], dz_s.at[o], dz_r.at[o], ctx=far_dev[o])
        copy.start()
        dz_copies.append(copy)
    dkv_r[seg] = dkv_p[seg]

    dq = (dot(dscore, keys, NN) * scale).astype(BF16)
    back = jnp.concatenate(
        [attended[j * sel : (j + 1) * sel] for j in range(group)]
        + [dq[j * sel : (j + 1) * sel] for j in range(group)],
        axis=1,
    )
    sback[...] = dot(pick, back, TN).astype(BF16).reshape(SEG_DEV, pad, 2 * gw)
    b_copies = []
    for o in order:
        copy = remote(
            sback.at[mate[o], pl.ds(0, cap)], rback.at[g], b_s.at[o], b_r.at[o], ctx=plane[o]
        )
        copy.start()
        b_copies.append(copy)
    rback[g] = sback[g, 0:cap]

    for copy in dz_copies:
        copy.wait_recv()
    dkv = dkv_r[0]
    for s in range(1, n_seg):
        dkv = dkv + dkv_r[s]
    skb[...] = dot(pick, dkv.astype(BF16), TN).astype(BF16).reshape(SEG_DEV, pad, 2 * head)
    kb_copies = []
    for o in order:
        copy = remote(
            skb.at[mate[o], pl.ds(0, cap)], rkb.at[g], kb_s.at[o], kb_r.at[o], ctx=plane[o]
        )
        copy.start()
        kb_copies.append(copy)
    rkb[g] = skb[g, 0:cap]

    def norm_back(grad, unit, inv, gain):
        turned = rot(grad.astype(F32), -1)
        term = jnp.sum(turned * unit, axis=0, keepdims=True)
        scaled = turned * gain
        mean = jnp.mean(scaled * unit, axis=-1, keepdims=True)
        return (inv * (scaled - unit * mean)).astype(BF16), term

    term_q = jnp.zeros((1, head), F32)
    logit = jnp.zeros((cap, head), F32)
    for o, copy in zip((0, 1, 2, 3), (None, b_copies[2], b_copies[0], b_copies[1])):
        if copy is not None:
            copy.wait_recv()
        t = mate[o]
        for j in range(group):
            cols = pl.ds(pl.multiple_of(t * gw + j * head, head), head)
            att = rback[t, :, j * head : (j + 1) * head].astype(F32)
            out_ref[:, cols] = (gate * att).astype(BF16)
            logit = logit + dround[t * group + j].astype(F32) * att
            grad, term = norm_back(
                rback[t, :, gw + j * head : gw + (j + 1) * head],
                qunit[t * group + j],
                qinv[t * group + j],
                gain_q,
            )
            gq_ref[:, cols] = grad
            term_q = term_q + term
    gl_ref[...] = (1.0 - gate) * jnp.sum(logit, axis=-1, keepdims=True)

    for copy in kb_copies:
        copy.wait_recv()
    term_k = jnp.zeros((1, head), F32)
    for t in range(heads_k):
        cols = pl.ds(t * head, head)
        grad, term = norm_back(rkb[t, :, 0:head], kunit[t], kinv[t], gain_k)
        gk_ref[:, cols] = grad
        gv_ref[:, cols] = rkb[t, :, head:]
        term_k = term_k + term

    which = lax.broadcasted_iota(jnp.int32, (8, head), 0)
    terms = jnp.where(which == 0, term_q, jnp.where(which == 1, term_k, 0.0))
    last = []
    gplane[g] = terms
    stage = []
    for o in order:
        copy = remote(gplane.at[g], gplane.at[g], g_s.at[o], g_r.at[o], ctx=plane[o])
        copy.start()
        stage.append(copy)
    for copy in stage:
        copy.wait_recv()
    last += stage
    terms = gplane[0] + gplane[1] + gplane[2] + gplane[3]
    gseg[seg] = terms
    stage = []
    for o in far:
        copy = remote(gseg.at[seg], gseg.at[seg], g_s.at[3 + o], g_r.at[3 + o], ctx=far_dev[o])
        copy.start()
        stage.append(copy)
    for copy in stage:
        copy.wait_recv()
    last += stage
    terms = gseg[0]
    for s in range(1, n_seg):
        terms = terms + gseg[s]
    gdp[my_dp] = terms
    stage = []
    for o in rows_dp:
        at = 3 + n_seg - 1 + o
        copy = remote(gdp.at[my_dp], gdp.at[my_dp], g_s.at[at], g_r.at[at], dp=rows_dp[o])
        copy.start()
        stage.append(copy)
    for copy in stage:
        copy.wait_recv()
    last += stage
    terms = gdp[0]
    for s in range(1, n_dp):
        terms = terms + gdp[s]
    selected_all = n_dp * total
    over_q = 1.0 / math.sqrt(selected_all * group * heads_k)
    over_k = 1.0 / math.sqrt(selected_all * heads_k)
    gains_ref[...] = terms * jnp.where(which == 0, over_q, over_k)

    for copy in kv_copies + qd_copies + z_copies + dz_copies + b_copies + kb_copies + last:
        copy.wait_send()


def per_device(
    n_seg,
    n_dp,
    positions,
    queries,
    keys,
    values,
    router_logits,
    out_cotangent,
    query_gain,
    key_gain,
):
    cap = positions.shape[1]
    head = query_gain.shape[0]
    width_q = queries.shape[2]
    width_k = keys.shape[2]
    heads_q = width_q // head
    heads_k = width_k // head
    gw = width_q // heads_k
    sel = SEL_DEV * SEG_DEV
    pad = sel
    pos = positions[0]
    half = jnp.arange(head // 2).astype(F32)
    frequency = jnp.exp(half * (-2.0 * math.log(rope_base) / head))
    angles = pos.astype(F32)[:, None] * frequency[None, :]
    cos = jnp.cos(angles)
    sin = jnp.sin(angles)
    gating = jax.nn.sigmoid(router_logits[0])
    live = (pos >= 0).astype(F32)
    aux = jnp.stack(
        [
            jnp.concatenate([cos, cos], axis=1),
            jnp.concatenate([-sin, sin], axis=1),
            jnp.broadcast_to(gating[:, None], (cap, head)),
            jnp.broadcast_to(live[:, None], (cap, head)),
        ]
    )
    gains = jnp.stack([query_gain, key_gain])
    vmem = pl.BlockSpec(memory_space=pltpu.VMEM)
    dma = pltpu.SemaphoreType.DMA
    n_g = 4 + n_seg - 1 + n_dp
    out, gq, gk, gv, gl, gsum = pl.pallas_call(
        functools.partial(kernel, n_seg, n_dp),
        out_shape=(
            jax.ShapeDtypeStruct((cap, width_q), BF16),
            jax.ShapeDtypeStruct((cap, width_q), BF16),
            jax.ShapeDtypeStruct((cap, width_k), BF16),
            jax.ShapeDtypeStruct((cap, width_k), BF16),
            jax.ShapeDtypeStruct((cap, head), F32),
            jax.ShapeDtypeStruct((8, head), F32),
        ),
        in_specs=[vmem] * 6,
        out_specs=(vmem,) * 6,
        scratch_shapes=[
            pltpu.VMEM((SEG_DEV, pad, 2 * head), BF16),
            pltpu.VMEM((SEG_DEV, pad, 2 * head), BF16),
            pltpu.VMEM((SEG_DEV - 1, cap, 2 * gw), BF16),
            pltpu.VMEM((SEG_DEV, pad, 2 * gw), BF16),
            pltpu.VMEM((heads_q, cap, head), F32),
            pltpu.VMEM((heads_q, cap, head), F32),
            pltpu.VMEM((heads_q, cap, head), BF16),
            pltpu.VMEM((heads_k, cap, head), F32),
            pltpu.VMEM((heads_k, cap, head), F32),
            pltpu.VMEM((n_seg, sel, 2 * head), BF16),
            pltpu.VMEM((n_seg, sel, 2 * head), F32),
            pltpu.VMEM((n_seg, sel, 2 * head), F32),
            pltpu.VMEM((SEG_DEV, pad, 2 * gw), BF16),
            pltpu.VMEM((SEG_DEV, cap, 2 * gw), BF16),
            pltpu.VMEM((SEG_DEV, pad, 2 * head), BF16),
            pltpu.VMEM((SEG_DEV, cap, 2 * head), BF16),
            pltpu.VMEM((SEG_DEV, 8, head), F32),
            pltpu.VMEM((n_seg, 8, head), F32),
            pltpu.VMEM((n_dp, 8, head), F32),
            dma((SEG_DEV,)),
            dma((SEG_DEV,)),
            dma((SEG_DEV,)),
            dma((SEG_DEV,)),
            dma((n_seg,)),
            dma((n_seg,)),
            dma((n_seg,)),
            dma((n_seg,)),
            dma((SEG_DEV,)),
            dma((SEG_DEV,)),
            dma((SEG_DEV,)),
            dma((SEG_DEV,)),
            dma((n_g,)),
            dma((n_g,)),
        ],
        compiler_params=pltpu.CompilerParams(
            collective_id=0, has_side_effects=True, vmem_limit_bytes=40 * 1024 * 1024
        ),
    )(aux, queries[0], keys[0], values[0], out_cotangent[0], gains)
    return (out[None], gq[None], gk[None], gv[None], gl[:, 0][None], gsum[0], gsum[1])


def solution(mesh):
    n_seg = mesh.shape["ctx"] // SEG_DEV
    n_dp = mesh.shape["dp"]
    return jax.shard_map(
        functools.partial(per_device, n_seg, n_dp),
        mesh=mesh,
        in_specs=(
            P("dp", "ctx"),
            P("dp", "ctx", None),
            P("dp", "ctx", None),
            P("dp", "ctx", None),
            P("dp", "ctx"),
            P("dp", "ctx", None),
            P(),
            P(),
        ),
        out_specs=(
            P("dp", "ctx", None),
            P("dp", "ctx", None),
            P("dp", "ctx", None),
            P("dp", "ctx", None),
            P("dp", "ctx"),
            P(),
            P(),
        ),
        check_vma=False,
    )
```

time: 224 us -> 44.6 us (0.20)
  blocking collectives: 88.4 us -> 0 us
  waiting for transfers between devices: 72.4 us -> 0 us
  Pallas kernels: 0 us -> 35.7 us
  starting transfers between devices: 19.3 us -> 0 us
  between operations: 14.7 us -> 0.69 us
  other arithmetic: 15.6 us -> 2.31 us
  matrix products: 5.42 us -> 0 us
    reduce_scatter x1 -> x0, waiting for transfers between devices: 54.3 us -> none  [per_device(): lax.psum_scatter(key_term(jnp.int32(0), per_owner * lax.axis_size('ctx'))...]
    psum x1 -> x0, blocking collectives: 40.2 us -> none  [per_device(): gain_sums = lax.psum((query_term, key_term_sum), ('dp', 'ctx'))]
    pallas_call x0 -> x1, Pallas kernels: none -> 35.7 us  [per_device(): pl.pallas_call(functools.partial(kernel, n_seg, n_dp), out_shape=(jax.Sha...]
    all_gather x1 -> x0, blocking collectives: 34.6 us -> none  [per_device(): keys_all = lax.all_gather(kv_rows, 'ctx', axis=0, tiled=True)]
    ppermute x8 -> x0, starting transfers between devices: 19.3 us -> none  [shifted(): return lax.ppermute(value, axis, pairs)]
    ppermute x8 -> x0, waiting for transfers between devices: 18.2 us -> none  [shifted(): return lax.ppermute(value, axis, pairs)]
    unnamed x1 -> x0, blocking collectives: 13.7 us -> none
    reduce_sum x10 -> x0, other arithmetic: 5.12 us -> none  [the longest x4 1.66 us: norm_grad(): gain_term = jnp.sum(unrotated * unit_rows, axis=(0, 1))]
  transfers between devices with their start and end apart: 9 -> 0, of which waited for: 4 -> 0; matrix products, arithmetic and copies ran while one was open for 1% -> 0% of each run, Pallas kernels for 0% -> 0%
where the time goes in v1:
time: 44.6 us; the launch traced here: 44.4 us
  Pallas kernels  35.7 us (80%)
  local copies, waits for them, and re-layouts  5.7 us (13%)
  other arithmetic  2.31 us (5%)
  between operations  0.69 us (2%)
    pallas_call x1, Pallas kernels, per_device(): pl.pallas_call(functools.partial(kernel, n_seg, n_dp), out_shape=(jax.Sha...  35.7 us
    unnamed x16, local copies, waits for them, and re-layouts  4.41 us

profile of v1, /device:TPU:0, one launch (start us, length us, event | category | flops | bytes accessed | tf_op | source)
XLA Modules:
  0.0 44.4 jit_solution(8946400350404728011)
XLA Ops:
  0.6 0.0 copy-start
  0.6 0.7 %convert_bitcast_fusion = f32[48]{0:T(128)S(1)} fusion(s32[1,48]{1,0:T(1,128)} %param.8), kind=kLoop, calls=%fused_computation.14 | loop fusion | flops 48 | bytes 384 | tf_op jit(solution)/shard_map/convert_element_type | solution.py:376
  1.4 0.2 multiply_cosine_fusion
  1.5 0.1 maximum_bitcast_fusion
  1.6 0.7 %divide_bitcast_fusion = f32[48]{0:T(128)S(1)} fusion(f32[1,48]{1,0:T(1,128)} %param.12), kind=kLoop, calls=%fused_computation.12 | loop fusion | flops 144 | bytes 384 | tf_op jit(solution)/shard_map/div | solution.py:379
  2.3 0.1 stack_broadcast_in_dim.4
  2.4 0.7 %fusion.1 = f32[48]{0:T(128)S(1)} fusion(s32[1,48]{1,0:T(1,128)} %param.8), kind=kLoop, calls=%fused_computation.9 | loop fusion | flops 96 | bytes 384 | tf_op jit(solution)/shard_map/convert_element_type | solution.py:380
  3.0 0.1 stack_broadcast_in_dim.5
  3.1 0.0 copy-start.2
  3.1 0.0 copy-start.4
  3.1 0.0 copy-start.5
  3.1 0.7 %copy-done.4 = f32[128]{0:T(128)S(1)} copy-done((f32[128]{0:T(128)S(1)}, f32[128]{0:T(128)}, u32[]{:S(2)}) %copy-start.4) | copy-done | bytes 536
  3.8 0.0 copy-done.5
  3.8 0.0 copy-done
  3.8 0.1 copy-done.2
  3.9 0.0 copy-done.3
  3.9 1.0 %copy-done.1 = bf16[1,48,3072]{2,1,0:T(8,128)(2,1)S(1)} copy-done((bf16[1,48,3072]{2,1,0:T(8,128)(2,1)S(1)}, bf16[1,48,3072]{2,1,0:T(8,128)(2,1)}, u32[]{:S(2)}) %copy-start.1) | copy-done | bytes 294936
  4.9 35.7 %shard_map.135 = (bf16[48,3072]{1,0:T(8,128)(2,1)S(1)}, bf16[48,3072]{1,0:T(8,128)(2,1)S(1)}, bf16[48,512]{1,0:T(8,128)(2,1)S(1)}, bf16[48,512]{1,0:T(8,128)(2,1...) custom-call(f32[4,48,128]{2,1,0:T(8,128)S(1)} %pad_maximum_fusion.aux_ref, bf16[48,3072]{1,0:T(8,128)(2,1)S(1)} %bitcast.25, ...), custom_call_target="tpu_custom_call" | custom-call | tf_op jit(solution)/shard_map/pallas_call | solution.py:393
  40.6 0.5 %slice_bitcast_fusion = (f32[128]{0:T(128)}, f32[128]{0:T(128)}) fusion(f32[8,128]{1,0:T(8,128)S(1)} %get-tuple-element.18), kind=kLoop, calls=%fused_computation.10 | loop fusion | bytes 2048 | tf_op jit(solution)/shard_map/squeeze | solution.py:444
  41.1 0.6 %slice_reduce_fusion = f32[48]{0:T(128)} fusion(f32[48,128]{1,0:T(8,128)S(1)} %get-tuple-element.17), kind=kLoop, calls=%fused_computation.5 | loop fusion | bytes 384 | tf_op jit(solution)/shard_map/slice | solution.py:444
  41.7 0.7 %copy.19 = bf16[1,48,3072]{2,1,0:T(8,128)(2,1)} copy(bf16[1,48,3072]{2,1,0:T(8,128)(2,1)S(1)} %bitcast.28) | data formatting | bytes 589824
  42.5 0.7 %copy.20 = bf16[1,48,3072]{2,1,0:T(8,128)(2,1)} copy(bf16[1,48,3072]{2,1,0:T(8,128)(2,1)S(1)} %bitcast.27) | data formatting | bytes 589824
  43.2 0.6 %copy.21 = bf16[1,48,512]{2,1,0:T(8,128)(2,1)} copy(bf16[1,48,512]{2,1,0:T(8,128)(2,1)S(1)} %bitcast.32) | data formatting | bytes 98304
  43.8 0.6 %copy.22 = bf16[1,48,512]{2,1,0:T(8,128)(2,1)} copy(bf16[1,48,512]{2,1,0:T(8,128)(2,1)S(1)} %bitcast.31) | data formatting | bytes 98304
  (5 shorter events, 0.0 us)
Async XLA Ops:
  0.6 3.2 %copy-start = (bf16[1,48,3072]{2,1,0:T(8,128)(2,1)S(1)}, bf16[1,48,3072]{2,1,0:T(8,128)(2,1)}, u32[]{:S(2)}) copy-start(bf16[1,48,3072]{2,1,0:T(8,128)(2,1)} %param.9) | copy-start | bytes 884740
  3.1 0.8 %copy-start.2 = (bf16[1,48,512]{2,1,0:T(8,128)(2,1)S(1)}, bf16[1,48,512]{2,1,0:T(8,128)(2,1)}, u32[]{:S(2)}) copy-start(bf16[1,48,512]{2,1,0:T(8,128)(2,1)} %param.10) | copy-start | bytes 147460
  3.1 0.8 %copy-start.3 = (bf16[1,48,512]{2,1,0:T(8,128)(2,1)S(1)}, bf16[1,48,512]{2,1,0:T(8,128)(2,1)}, u32[]{:S(2)}) copy-start(bf16[1,48,512]{2,1,0:T(8,128)(2,1)} %param.11) | copy-start | bytes 147460
  3.1 0.7 %copy-start.4 = (f32[128]{0:T(128)S(1)}, f32[128]{0:T(128)}, u32[]{:S(2)}) copy-start(f32[128]{0:T(128)} %param.15) | copy-start | bytes 1540
  3.1 0.7 %copy-start.5 = (f32[128]{0:T(128)S(1)}, f32[128]{0:T(128)}, u32[]{:S(2)}) copy-start(f32[128]{0:T(128)} %param.14) | copy-start | bytes 1540
  3.9 1.0 %copy-start.1 = (bf16[1,48,3072]{2,1,0:T(8,128)(2,1)S(1)}, bf16[1,48,3072]{2,1,0:T(8,128)(2,1)}, u32[]{:S(2)}) copy-start(bf16[1,48,3072]{2,1,0:T(8,128)(2,1)} %param.13) | copy-start | bytes 884740

commit v2 on v1

--- a/solution.py
+++ b/solution.py
@@ -3,6 +3,7 @@
 
 import jax
 import jax.numpy as jnp
+import numpy as np
 from jax import lax
 from jax.experimental import pallas as pl
 from jax.experimental.pallas import tpu as pltpu
@@ -30,7 +31,8 @@
 def kernel(
     n_seg,
     n_dp,
-    aux_ref,
+    pos_ref,
+    logit_ref,
     q_ref,
     k_ref,
     v_ref,
@@ -41,11 +43,14 @@
     gk_ref,
     gv_ref,
     gl_ref,
-    gains_ref,
+    gains_q_ref,
+    gains_k_ref,
     skv,
     rkv,
-    sqd,
-    rqd,
+    sq,
+    rq,
+    sd,
+    rd,
     qunit,
     qinv,
     dround,
@@ -54,23 +59,28 @@
     kv_all,
     dkv_p,
     dkv_r,
-    sback,
-    rback,
+    satt,
+    ratt,
+    sdq,
+    rdq,
     skb,
     rkb,
     gplane,
-    gseg,
-    gdp,
+    gall,
     kv_s,
     kv_r,
-    qd_s,
-    qd_r,
+    q_s,
+    q_r,
+    d_s,
+    d_r,
     z_s,
     z_r,
     dz_s,
     dz_r,
     b_s,
     b_r,
+    e_s,
+    e_r,
     kb_s,
     kb_r,
     g_s,
@@ -94,7 +104,9 @@
     plane = {o: seg * SEG_DEV + mate[o] for o in (1, 2, 3)}
     far = {o: (seg + o) % n_seg for o in range(1, n_seg)}
     far_dev = {o: far[o] * SEG_DEV + g for o in far}
-    rows_dp = {o: (my_dp + o) % n_dp for o in range(1, n_dp)}
+    cells = n_dp * n_seg
+    cell = my_dp * n_seg + seg
+    others = {o: (cell + o) % cells for o in range(1, cells)}
     order = (2, 3, 1)
 
     def remote(src, dst, ssem, rsem, ctx=None, dp=None):
@@ -109,15 +121,24 @@
 
     barrier = pltpu.get_barrier_semaphore()
     peers = [(my_dp, plane[o]) for o in order]
-    peers += [(my_dp, far_dev[o]) for o in far]
-    peers += [(rows_dp[o], my_ctx) for o in rows_dp]
+    peers += [(c // n_seg, c % n_seg * SEG_DEV + g) for c in others.values()]
     for peer in peers:
         pl.semaphore_signal(barrier, inc=1, device_id=peer, device_id_type=pl.DeviceIdType.MESH)
 
-    cos = aux_ref[0]
-    sin = aux_ref[1]
-    gate = aux_ref[2]
-    valid = aux_ref[3]
+    eye = lax.broadcasted_iota(jnp.int32, (cap, cap), 0) == lax.broadcasted_iota(
+        jnp.int32, (cap, cap), 1
+    )
+
+    def column(line):
+        return jnp.sum(jnp.where(eye, line, 0.0), axis=1, keepdims=True)
+
+    pos = jnp.broadcast_to(column(pos_ref[...].astype(F32)), (cap, head))
+    valid = jnp.where(pos >= 0.0, 1.0, 0.0)
+    angle = pos * gain_ref[2:3]
+    cos = jnp.cos(angle)
+    sin = jnp.sin(angle)
+    sin = jnp.where(lax.broadcasted_iota(jnp.int32, (cap, head), 1) < head // 2, -sin, sin)
+    gate = jax.nn.sigmoid(jnp.broadcast_to(column(logit_ref[...]), (cap, head)))
     gain_q = gain_ref[0:1]
     gain_k = gain_ref[1:2]
 
@@ -149,7 +170,8 @@
         kv_copies.append(copy)
     rkv[g] = skv[g]
 
-    qd_copies = []
+    q_copies = []
+    d_copies = []
     for o in order + (0,):
         t = mate[o]
         for j in range(group):
@@ -158,22 +180,35 @@
             qunit[t * group + j] = unit
             qinv[t * group + j] = jnp.broadcast_to(inv, (cap, head))
             turned = rot(unit * gain_q, 1).astype(BF16)
+            if o == 0:
+                rq[g, 0:cap, j * head : (j + 1) * head] = turned
+            else:
+                sq[o - 1, :, j * head : (j + 1) * head] = turned
+        if o != 0:
+            copy = remote(
+                sq.at[o - 1], rq.at[g, pl.ds(0, cap)], q_s.at[o], q_r.at[o], ctx=plane[o]
+            )
+            copy.start()
+            q_copies.append(copy)
+    for o in order + (0,):
+        t = mate[o]
+        for j in range(group):
+            cols = pl.ds(pl.multiple_of(t * gw + j * head, head), head)
             weighted = (gate * c_ref[:, cols].astype(F32)).astype(BF16)
             dround[t * group + j] = weighted
             if o == 0:
-                rqd[g, 0:cap, j * head : (j + 1) * head] = turned
-                rqd[g, 0:cap, gw + j * head : gw + (j + 1) * head] = weighted
+                rd[g, 0:cap, j * head : (j + 1) * head] = weighted
             else:
-                sqd[o - 1, :, j * head : (j + 1) * head] = turned
-                sqd[o - 1, :, gw + j * head : gw + (j + 1) * head] = weighted
+                sd[o - 1, :, j * head : (j + 1) * head] = weighted
         if o != 0:
             copy = remote(
-                sqd.at[o - 1], rqd.at[g, pl.ds(0, cap)], qd_s.at[o], qd_r.at[o], ctx=plane[o]
+                sd.at[o - 1], rd.at[g, pl.ds(0, cap)], d_s.at[o], d_r.at[o], ctx=plane[o]
             )
             copy.start()
-            qd_copies.append(copy)
+            d_copies.append(copy)
     for m in range(SEG_DEV):
-        rqd[m, cap:, :] = jnp.zeros((pad - cap, 2 * gw), BF16)
+        rq[m, cap:, :] = jnp.zeros((pad - cap, gw), BF16)
+        rd[m, cap:, :] = jnp.zeros((pad - cap, gw), BF16)
 
     for copy in kv_copies:
         copy.wait_recv()
@@ -199,13 +234,17 @@
         copy.start()
         z_copies.append(copy)
 
-    for copy in qd_copies:
-        copy.wait_recv()
-    qd = dot(pick, rqd[...].reshape(wide, 2 * gw), NN).astype(BF16)
-    q_rows = jnp.concatenate([qd[:, j * head : (j + 1) * head] for j in range(group)], axis=0)
-    d_rows = jnp.concatenate(
-        [qd[:, gw + j * head : gw + (j + 1) * head] for j in range(group)], axis=0
-    )
+    def heads_down(wide_rows):
+        return jnp.concatenate(
+            [wide_rows[:, j * head : (j + 1) * head] for j in range(group)], axis=0
+        )
+
+    def heads_across(tall_rows):
+        return jnp.concatenate([tall_rows[j * sel : (j + 1) * sel] for j in range(group)], axis=1)
+
+    for copy in q_copies:
+        copy.wait_recv()
+    q_rows = heads_down(dot(pick, rq[...].reshape(wide, gw), NN).astype(BF16))
     for copy in z_copies:
         copy.wait_recv()
 
@@ -221,6 +260,19 @@
     probs = exps / jnp.sum(exps, axis=-1, keepdims=True)
     probs_b = probs.astype(BF16)
     attended = dot(probs_b, vals, NN).astype(BF16)
+    satt[...] = dot(pick, heads_across(attended), TN).astype(BF16).reshape(SEG_DEV, pad, gw)
+    b_copies = []
+    for o in order:
+        copy = remote(
+            satt.at[mate[o], pl.ds(0, cap)], ratt.at[g], b_s.at[o], b_r.at[o], ctx=plane[o]
+        )
+        copy.start()
+        b_copies.append(copy)
+    ratt[g] = satt[g, 0:cap]
+
+    for copy in d_copies:
+        copy.wait_recv()
+    d_rows = heads_down(dot(pick, rd[...].reshape(wide, gw), NN).astype(BF16))
     delta = jnp.sum(d_rows.astype(F32) * attended.astype(F32), axis=-1, keepdims=True)
     dprob = dot(d_rows, vals, NT)
     dscore = (probs * (dprob - delta)).astype(BF16)
@@ -234,20 +286,50 @@
     dkv_r[seg] = dkv_p[seg]
 
     dq = (dot(dscore, keys, NN) * scale).astype(BF16)
-    back = jnp.concatenate(
-        [attended[j * sel : (j + 1) * sel] for j in range(group)]
-        + [dq[j * sel : (j + 1) * sel] for j in range(group)],
-        axis=1,
-    )
-    sback[...] = dot(pick, back, TN).astype(BF16).reshape(SEG_DEV, pad, 2 * gw)
-    b_copies = []
+    sdq[...] = dot(pick, heads_across(dq), TN).astype(BF16).reshape(SEG_DEV, pad, gw)
+    e_copies = []
     for o in order:
         copy = remote(
-            sback.at[mate[o], pl.ds(0, cap)], rback.at[g], b_s.at[o], b_r.at[o], ctx=plane[o]
+            sdq.at[mate[o], pl.ds(0, cap)], rdq.at[g], e_s.at[o], e_r.at[o], ctx=plane[o]
         )
         copy.start()
-        b_copies.append(copy)
-    rback[g] = sback[g, 0:cap]
+        e_copies.append(copy)
+    rdq[g] = sdq[g, 0:cap]
+
+    logit = jnp.zeros((cap, head), F32)
+    for copy in b_copies:
+        copy.wait_recv()
+    for t in range(SEG_DEV):
+        for j in range(group):
+            cols = pl.ds(t * gw + j * head, head)
+            att = ratt[t, :, j * head : (j + 1) * head].astype(F32)
+            out_ref[:, cols] = (gate * att).astype(BF16)
+            logit = logit + dround[t * group + j].astype(F32) * att
+    total_logit = (1.0 - gate[:, 0:1]) * jnp.sum(logit, axis=-1, keepdims=True)
+    gl_ref[...] = jnp.sum(jnp.where(eye, total_logit, 0.0), axis=0, keepdims=True)
+
+    def norm_back(grad, unit, inv, gain):
+        turned = rot(grad.astype(F32), -1)
+        term = jnp.sum(turned * unit, axis=0, keepdims=True)
+        scaled = turned * gain
+        mean = jnp.mean(scaled * unit, axis=-1, keepdims=True)
+        return (inv * (scaled - unit * mean)).astype(BF16), term
+
+    def query_back(o, term_q):
+        t = mate[o]
+        for j in range(group):
+            cols = pl.ds(pl.multiple_of(t * gw + j * head, head), head)
+            grad, term = norm_back(
+                rdq[t, :, j * head : (j + 1) * head],
+                qunit[t * group + j],
+                qinv[t * group + j],
+                gain_q,
+            )
+            gq_ref[:, cols] = grad
+            term_q = term_q + term
+        return term_q
+
+    term_q = query_back(0, jnp.zeros((1, head), F32))
 
     for copy in dz_copies:
         copy.wait_recv()
@@ -264,33 +346,9 @@
         kb_copies.append(copy)
     rkb[g] = skb[g, 0:cap]
 
-    def norm_back(grad, unit, inv, gain):
-        turned = rot(grad.astype(F32), -1)
-        term = jnp.sum(turned * unit, axis=0, keepdims=True)
-        scaled = turned * gain
-        mean = jnp.mean(scaled * unit, axis=-1, keepdims=True)
-        return (inv * (scaled - unit * mean)).astype(BF16), term
-
-    term_q = jnp.zeros((1, head), F32)
-    logit = jnp.zeros((cap, head), F32)
-    for o, copy in zip((0, 1, 2, 3), (None, b_copies[2], b_copies[0], b_copies[1])):
-        if copy is not None:
-            copy.wait_recv()
-        t = mate[o]
-        for j in range(group):
-            cols = pl.ds(pl.multiple_of(t * gw + j * head, head), head)
-            att = rback[t, :, j * head : (j + 1) * head].astype(F32)
-            out_ref[:, cols] = (gate * att).astype(BF16)
-            logit = logit + dround[t * group + j].astype(F32) * att
-            grad, term = norm_back(
-                rback[t, :, gw + j * head : gw + (j + 1) * head],
-                qunit[t * group + j],
-                qinv[t * group + j],
-                gain_q,
-            )
-            gq_ref[:, cols] = grad
-            term_q = term_q + term
-    gl_ref[...] = (1.0 - gate) * jnp.sum(logit, axis=-1, keepdims=True)
+    for o, copy in zip((1, 2, 3), (e_copies[2], e_copies[0], e_copies[1])):
+        copy.wait_recv()
+        term_q = query_back(o, term_q)
 
     for copy in kb_copies:
         copy.wait_recv()
@@ -315,38 +373,46 @@
         copy.wait_recv()
     last += stage
     terms = gplane[0] + gplane[1] + gplane[2] + gplane[3]
-    gseg[seg] = terms
+    gall[cell] = terms
     stage = []
-    for o in far:
-        copy = remote(gseg.at[seg], gseg.at[seg], g_s.at[3 + o], g_r.at[3 + o], ctx=far_dev[o])
+    for o, c in others.items():
+        copy = remote(
+            gall.at[cell],
+            gall.at[cell],
+            g_s.at[3 + o],
+            g_r.at[3 + o],
+            ctx=c % n_seg * SEG_DEV + g,
+            dp=c // n_seg,
+        )
         copy.start()
         stage.append(copy)
     for copy in stage:
         copy.wait_recv()
     last += stage
-    terms = gseg[0]
-    for s in range(1, n_seg):
-        terms = terms + gseg[s]
-    gdp[my_dp] = terms
-    stage = []
-    for o in rows_dp:
-        at = 3 + n_seg - 1 + o
-        copy = remote(gdp.at[my_dp], gdp.at[my_dp], g_s.at[at], g_r.at[at], dp=rows_dp[o])
-        copy.start()
-        stage.append(copy)
-    for copy in stage:
-        copy.wait_recv()
-    last += stage
-    terms = gdp[0]
-    for s in range(1, n_dp):
-        terms = terms + gdp[s]
+    terms = gall[0]
+    for s in range(1, cells):
+        terms = terms + gall[s]
     selected_all = n_dp * total
     over_q = 1.0 / math.sqrt(selected_all * group * heads_k)
     over_k = 1.0 / math.sqrt(selected_all * heads_k)
-    gains_ref[...] = terms * jnp.where(which == 0, over_q, over_k)
-
-    for copy in kv_copies + qd_copies + z_copies + dz_copies + b_copies + kb_copies + last:
+    gains_q_ref[...] = terms[0:1] * over_q
+    gains_k_ref[...] = terms[1:2] * over_k
+
+    mine = kv_copies + q_copies + d_copies + z_copies + dz_copies
+    for copy in mine + b_copies + e_copies + kb_copies + last:
         copy.wait_send()
+
+
+def place_results(*refs):
+    sems = refs[-1]
+    half = len(refs) // 2
+    copies = [
+        pltpu.make_async_copy(refs[i], refs[half + i], sems.at[i]) for i in range(half)
+    ]
+    for copy in copies:
+        copy.start()
+    for copy in copies:
+        copy.wait()
 
 
 def per_device(
@@ -370,43 +436,32 @@
     gw = width_q // heads_k
     sel = SEL_DEV * SEG_DEV
     pad = sel
-    pos = positions[0]
-    half = jnp.arange(head // 2).astype(F32)
-    frequency = jnp.exp(half * (-2.0 * math.log(rope_base) / head))
-    angles = pos.astype(F32)[:, None] * frequency[None, :]
-    cos = jnp.cos(angles)
-    sin = jnp.sin(angles)
-    gating = jax.nn.sigmoid(router_logits[0])
-    live = (pos >= 0).astype(F32)
-    aux = jnp.stack(
-        [
-            jnp.concatenate([cos, cos], axis=1),
-            jnp.concatenate([-sin, sin], axis=1),
-            jnp.broadcast_to(gating[:, None], (cap, head)),
-            jnp.broadcast_to(live[:, None], (cap, head)),
-        ]
-    )
-    gains = jnp.stack([query_gain, key_gain])
+    steps = np.arange(head // 2, dtype=np.float64) * (-2.0 * math.log(rope_base) / head)
+    frequency = np.tile(np.exp(steps), 2).astype(np.float32)
+    gains = jnp.stack([query_gain, key_gain, jnp.asarray(frequency)])
     vmem = pl.BlockSpec(memory_space=pltpu.VMEM)
     dma = pltpu.SemaphoreType.DMA
-    n_g = 4 + n_seg - 1 + n_dp
-    out, gq, gk, gv, gl, gsum = pl.pallas_call(
+    n_g = 3 + n_seg * n_dp
+    results = pl.pallas_call(
         functools.partial(kernel, n_seg, n_dp),
         out_shape=(
             jax.ShapeDtypeStruct((cap, width_q), BF16),
             jax.ShapeDtypeStruct((cap, width_q), BF16),
             jax.ShapeDtypeStruct((cap, width_k), BF16),
             jax.ShapeDtypeStruct((cap, width_k), BF16),
-            jax.ShapeDtypeStruct((cap, head), F32),
-            jax.ShapeDtypeStruct((8, head), F32),
+            jax.ShapeDtypeStruct((1, cap), F32),
+            jax.ShapeDtypeStruct((1, head), F32),
+            jax.ShapeDtypeStruct((1, head), F32),
         ),
-        in_specs=[vmem] * 6,
-        out_specs=(vmem,) * 6,
+        in_specs=[vmem] * 7,
+        out_specs=(vmem,) * 7,
         scratch_shapes=[
             pltpu.VMEM((SEG_DEV, pad, 2 * head), BF16),
             pltpu.VMEM((SEG_DEV, pad, 2 * head), BF16),
-            pltpu.VMEM((SEG_DEV - 1, cap, 2 * gw), BF16),
-            pltpu.VMEM((SEG_DEV, pad, 2 * gw), BF16),
+            pltpu.VMEM((SEG_DEV - 1, cap, gw), BF16),
+            pltpu.VMEM((SEG_DEV, pad, gw), BF16),
+            pltpu.VMEM((SEG_DEV - 1, cap, gw), BF16),
+            pltpu.VMEM((SEG_DEV, pad, gw), BF16),
             pltpu.VMEM((heads_q, cap, head), F32),
             pltpu.VMEM((heads_q, cap, head), F32),
             pltpu.VMEM((heads_q, cap, head), BF16),
@@ -415,13 +470,16 @@
             pltpu.VMEM((n_seg, sel, 2 * head), BF16),
             pltpu.VMEM((n_seg, sel, 2 * head), F32),
             pltpu.VMEM((n_seg, sel, 2 * head), F32),
-            pltpu.VMEM((SEG_DEV, pad, 2 * gw), BF16),
-            pltpu.VMEM((SEG_DEV, cap, 2 * gw), BF16),
+            pltpu.VMEM((SEG_DEV, pad, gw), BF16),
+            pltpu.VMEM((SEG_DEV, cap, gw), BF16),
+            pltpu.VMEM((SEG_DEV, pad, gw), BF16),
+            pltpu.VMEM((SEG_DEV, cap, gw), BF16),
             pltpu.VMEM((SEG_DEV, pad, 2 * head), BF16),
             pltpu.VMEM((SEG_DEV, cap, 2 * head), BF16),
             pltpu.VMEM((SEG_DEV, 8, head), F32),
-            pltpu.VMEM((n_seg, 8, head), F32),
-            pltpu.VMEM((n_dp, 8, head), F32),
+            pltpu.VMEM((n_seg * n_dp, 8, head), F32),
+            dma((SEG_DEV,)),
+            dma((SEG_DEV,)),
             dma((SEG_DEV,)),
             dma((SEG_DEV,)),
             dma((SEG_DEV,)),
@@ -430,6 +488,8 @@
             dma((n_seg,)),
             dma((n_seg,)),
             dma((n_seg,)),
+            dma((SEG_DEV,)),
+            dma((SEG_DEV,)),
             dma((SEG_DEV,)),
             dma((SEG_DEV,)),
             dma((SEG_DEV,)),
@@ -440,8 +500,25 @@
         compiler_params=pltpu.CompilerParams(
             collective_id=0, has_side_effects=True, vmem_limit_bytes=40 * 1024 * 1024
         ),
-    )(aux, queries[0], keys[0], values[0], out_cotangent[0], gains)
-    return (out[None], gq[None], gk[None], gv[None], gl[:, 0][None], gsum[0], gsum[1])
+    )(positions, router_logits, queries[0], keys[0], values[0], out_cotangent[0], gains)
+    count = len(results)
+    anywhere = pl.BlockSpec(memory_space=pl.ANY)
+    out, gq, gk, gv, gl, gain_q, gain_k = pl.pallas_call(
+        place_results,
+        out_shape=tuple(jax.ShapeDtypeStruct(r.shape, r.dtype) for r in results),
+        in_specs=[anywhere] * count,
+        out_specs=(anywhere,) * count,
+        scratch_shapes=[dma((count,))],
+    )(*results)
+    return (
+        out[None],
+        gq[None],
+        gk[None],
+        gv[None],
+        gl,
+        gain_q.reshape(head),
+        gain_k.reshape(head),
+    )
 
 
 def solution(mesh):

time: 44.6 us -> 65.3 us (1.46)
  Pallas kernels: 35.7 us -> 56.2 us
  local copies, waits for them, and re-layouts: 5.7 us -> 8.06 us
  other arithmetic: 2.31 us -> 0.01 us
    pallas_call x0 -> x1, Pallas kernels: none -> 22.1 us  [per_device(): pl.pallas_call(place_results, out_shape=tuple((jax.ShapeDtypeStruct(r.sha...]
    unnamed x16 -> x32, local copies, waits for them, and re-layouts: 4.41 us -> 8.06 us
    pallas_call x1, Pallas kernels: 35.7 us -> 34.2 us  [per_device(): pl.pallas_call(functools.partial(kernel, n_seg, n_dp), out_shape=(jax.Sha...]
    convert_element_type x2 -> x0, other arithmetic: 1.37 us -> none  [the longest x1 0.7 us: per_device(): angles = pos.astype(F32)[:, None] * frequency[None, :]]
    div x1 -> x0, other arithmetic: 0.67 us -> none  [per_device(): gating = jax.nn.sigmoid(router_logits[0])]
where the time goes in v2:
time: 65.3 us; the launch traced here: 65 us
  Pallas kernels  56.2 us (86%)
  local copies, waits for them, and re-layouts  8.06 us (12%)
  between operations  0.69 us (1%)
    pallas_call x1, Pallas kernels, per_device(): pl.pallas_call(functools.partial(kernel, n_seg, n_dp), out_shape=(jax.Sha...  34.2 us
    pallas_call x1, Pallas kernels, per_device(): pl.pallas_call(place_results, out_shape=tuple((jax.ShapeDtypeStruct(r.sha...  22.1 us
    unnamed x32, local copies, waits for them, and re-layouts  8.06 us

profile of v2, /device:TPU:0, one launch (start us, length us, event | category | flops | bytes accessed | tf_op | source)
XLA Modules:
  0.0 65.0 jit_solution(2996987793949814174)
XLA Ops:
  0.6 0.0 copy-start.13
  0.6 0.0 copy-start.14
  0.7 0.0 copy-start.15
  0.7 0.6 copy-done.13
  1.3 0.0 copy-done.14
  1.3 0.0 copy-done.15
  1.3 0.0 copy-start.11
  1.3 0.0 copy-start.12
  1.3 0.6 copy-done.11
  2.0 0.0 copy-done.12
  2.0 1.0 %copy-done = bf16[1,48,3072]{2,1,0:T(8,128)(2,1)S(1)} copy-done((bf16[1,48,3072]{2,1,0:T(8,128)(2,1)S(1)}, bf16[1,48,3072]{2,1,0:T(8,128)(2,1)}, u32[]{:S(2)}) %copy-start) | copy-done | bytes 294936
  3.0 1.0 %copy-done.1 = bf16[1,48,3072]{2,1,0:T(8,128)(2,1)S(1)} copy-done((bf16[1,48,3072]{2,1,0:T(8,128)(2,1)S(1)}, bf16[1,48,3072]{2,1,0:T(8,128)(2,1)}, u32[]{:S(2)}) %copy-start.1) | copy-done | bytes 294936
  3.9 0.8 %copy-done.6 = bf16[1,48,512]{2,1,0:T(8,128)(2,1)S(1)} copy-done((bf16[1,48,512]{2,1,0:T(8,128)(2,1)S(1)}, bf16[1,48,512]{2,1,0:T(8,128)(2,1)}, u32[]{:S(2)}) %copy-start.6) | copy-done | bytes 49176
  4.7 0.8 %copy-done.7 = bf16[1,48,512]{2,1,0:T(8,128)(2,1)S(1)} copy-done((bf16[1,48,512]{2,1,0:T(8,128)(2,1)S(1)}, bf16[1,48,512]{2,1,0:T(8,128)(2,1)}, u32[]{:S(2)}) %copy-start.7) | copy-done | bytes 49176
  5.5 34.2 %shard_map.144 = (bf16[48,3072]{1,0:T(8,128)(2,1)S(1)}, bf16[48,3072]{1,0:T(8,128)(2,1)S(1)}, bf16[48,512]{1,0:T(8,128)(2,1)S(1)}, bf16[48,512]{1,0:T(8,128)(2,1...) custom-call(s32[1,48]{1,0:T(1,128)S(1)} %copy-done.11, f32[1,48]{1,0:T(1,128)S(1)} %copy-done.12, ...), custom_call_target="tpu_custom_call" | custom-call | tf_op jit(solution)/shard_map/pallas_call | solution.py:445
  39.7 0.0 copy-start.2
  39.7 0.7 %copy-done.2 = bf16[48,3072]{1,0:T(8,128)(2,1)} copy-done((bf16[48,3072]{1,0:T(8,128)(2,1)}, bf16[48,3072]{1,0:T(8,128)(2,1)S(1)}, u32[]{:S(2)}) %copy-start.2) | copy-done | bytes 294936
  40.4 0.7 %copy-done.3 = bf16[48,3072]{1,0:T(8,128)(2,1)} copy-done((bf16[48,3072]{1,0:T(8,128)(2,1)}, bf16[48,3072]{1,0:T(8,128)(2,1)S(1)}, u32[]{:S(2)}) %copy-start.3) | copy-done | bytes 294936
  41.1 0.6 copy-done.4
  41.7 0.6 copy-done.5
  42.3 0.6 copy-done.8
  42.9 0.0 copy-done.9
  42.9 0.0 copy-done.10
  42.9 22.1 %shard_map.145 = (bf16[48,3072]{1,0:T(8,128)(2,1)}, bf16[48,3072]{1,0:T(8,128)(2,1)}, bf16[48,512]{1,0:T(8,128)(2,1)}, bf16[48,512]{1,0:T(8,128)(2,1)}, f32[1,48...) custom-call(bf16[48,3072]{1,0:T(8,128)(2,1)} %copy-done.2, bf16[48,3072]{1,0:T(8,128)(2,1)} %copy-done.3, ...), custom_call_target="tpu_custom_call" | custom-call | tf_op jit(solution)/shard_map/pallas_call | solution.py:506
  (11 shorter events, 0.0 us)
Async XLA Ops:
  0.6 0.7 %copy-start.13 = (f32[128]{0:T(128)S(1)}, f32[128]{0:T(128)}, u32[]{:S(2)}) copy-start(f32[128]{0:T(128)} %param.16) | copy-start | bytes 1540
  0.6 0.7 %copy-start.14 = (f32[128]{0:T(128)S(1)}, f32[128]{0:T(128)}, u32[]{:S(2)}) copy-start(f32[128]{0:T(128)} %param.15) | copy-start | bytes 1540
  0.7 0.7 %copy-start.15 = (f32[1,128]{1,0:T(1,128)S(1)}, f32[1,128]{1,0:T(1,128)}, u32[]{:S(2)}) copy-start(f32[1,128]{1,0:T(1,128)} %constant.9) | copy-start | bytes 1540
  1.3 0.7 %copy-start.11 = (s32[1,48]{1,0:T(1,128)S(1)}, s32[1,48]{1,0:T(1,128)}, u32[]{:S(2)}) copy-start(s32[1,48]{1,0:T(1,128)} %pos_ref.1) | copy-start | bytes 580
  1.3 0.7 %copy-start.12 = (f32[1,48]{1,0:T(1,128)S(1)}, f32[1,48]{1,0:T(1,128)}, u32[]{:S(2)}) copy-start(f32[1,48]{1,0:T(1,128)} %logit_ref.1) | copy-start | bytes 580
  2.0 1.0 %copy-start = (bf16[1,48,3072]{2,1,0:T(8,128)(2,1)S(1)}, bf16[1,48,3072]{2,1,0:T(8,128)(2,1)}, u32[]{:S(2)}) copy-start(bf16[1,48,3072]{2,1,0:T(8,128)(2,1)} %param.10) | copy-start | bytes 884740
  3.0 1.0 %copy-start.1 = (bf16[1,48,3072]{2,1,0:T(8,128)(2,1)S(1)}, bf16[1,48,3072]{2,1,0:T(8,128)(2,1)}, u32[]{:S(2)}) copy-start(bf16[1,48,3072]{2,1,0:T(8,128)(2,1)} %param.14) | copy-start | bytes 884740
  3.9 0.8 %copy-start.6 = (bf16[1,48,512]{2,1,0:T(8,128)(2,1)S(1)}, bf16[1,48,512]{2,1,0:T(8,128)(2,1)}, u32[]{:S(2)}) copy-start(bf16[1,48,512]{2,1,0:T(8,128)(2,1)} %param.11) | copy-start | bytes 147460
  4.7 0.8 %copy-start.7 = (bf16[1,48,512]{2,1,0:T(8,128)(2,1)S(1)}, bf16[1,48,512]{2,1,0:T(8,128)(2,1)}, u32[]{:S(2)}) copy-start(bf16[1,48,512]{2,1,0:T(8,128)(2,1)} %param.12) | copy-start | bytes 147460
  39.7 0.7 %copy-start.2 = (bf16[48,3072]{1,0:T(8,128)(2,1)}, bf16[48,3072]{1,0:T(8,128)(2,1)S(1)}, u32[]{:S(2)}) copy-start(bf16[48,3072]{1,0:T(8,128)(2,1)S(1)} %get-tuple-element.21.refs_0_) | copy-start | bytes 884740
  40.4 0.7 %copy-start.3 = (bf16[48,3072]{1,0:T(8,128)(2,1)}, bf16[48,3072]{1,0:T(8,128)(2,1)S(1)}, u32[]{:S(2)}) copy-start(bf16[48,3072]{1,0:T(8,128)(2,1)S(1)} %get-tuple-element.22.refs_1_) | copy-start | bytes 884740
  41.1 0.6 copy-start.4
  41.7 0.6 copy-start.5
  42.3 0.6 copy-start.8
  42.3 0.6 copy-start.9
  42.3 0.6 copy-start.10

commit v3 on v2

--- a/solution.py
+++ b/solution.py
@@ -31,13 +31,15 @@
 def kernel(
     n_seg,
     n_dp,
-    pos_ref,
-    logit_ref,
-    q_ref,
-    k_ref,
-    v_ref,
-    c_ref,
-    gain_ref,
+    pos_hbm,
+    logit_hbm,
+    q_hbm,
+    k_hbm,
+    v_hbm,
+    c_hbm,
+    gq_in_hbm,
+    gk_in_hbm,
+    freq_hbm,
     out_ref,
     gq_ref,
     gk_ref,
@@ -45,6 +47,16 @@
     gl_ref,
     gains_q_ref,
     gains_k_ref,
+    pos_ref,
+    logit_ref,
+    q_ref,
+    k_ref,
+    v_ref,
+    c_ref,
+    gq_in_ref,
+    gk_in_ref,
+    freq_ref,
+    in_s,
     skv,
     rkv,
     sq,
@@ -86,9 +98,23 @@
     g_s,
     g_r,
 ):
+    given = (
+        (pos_hbm, pos_ref),
+        (logit_hbm, logit_ref),
+        (freq_hbm, freq_ref),
+        (gk_in_hbm, gk_in_ref),
+        (k_hbm, k_ref),
+        (v_hbm, v_ref),
+        (gq_in_hbm, gq_in_ref),
+        (q_hbm, q_ref),
+        (c_hbm, c_ref),
+    )
+    loads = [pltpu.make_async_copy(a, b, in_s.at[i]) for i, (a, b) in enumerate(given)]
+    for load in loads:
+        load.start()
     cap, width_q = q_ref.shape
     width_k = k_ref.shape[1]
-    head = gain_ref.shape[1]
+    head = freq_ref.shape[1]
     heads_k = width_k // head
     group = width_q // width_k
     gw = group * head
@@ -132,15 +158,16 @@
     def column(line):
         return jnp.sum(jnp.where(eye, line, 0.0), axis=1, keepdims=True)
 
+    for load in loads[:6]:
+        load.wait()
     pos = jnp.broadcast_to(column(pos_ref[...].astype(F32)), (cap, head))
     valid = jnp.where(pos >= 0.0, 1.0, 0.0)
-    angle = pos * gain_ref[2:3]
+    angle = pos * freq_ref[...]
     cos = jnp.cos(angle)
     sin = jnp.sin(angle)
     sin = jnp.where(lax.broadcasted_iota(jnp.int32, (cap, head), 1) < head // 2, -sin, sin)
     gate = jax.nn.sigmoid(jnp.broadcast_to(column(logit_ref[...]), (cap, head)))
-    gain_q = gain_ref[0:1]
-    gain_k = gain_ref[1:2]
+    gain_k = gk_in_ref[...]
 
     def normed(x):
         inv = lax.rsqrt(jnp.mean(x * x, axis=-1, keepdims=True) + norm_eps)
@@ -172,6 +199,9 @@
 
     q_copies = []
     d_copies = []
+    for load in loads[6:8]:
+        load.wait()
+    gain_q = gq_in_ref[...]
     for o in order + (0,):
         t = mate[o]
         for j in range(group):
@@ -190,6 +220,7 @@
             )
             copy.start()
             q_copies.append(copy)
+    loads[8].wait()
     for o in order + (0,):
         t = mate[o]
         for j in range(group):
@@ -404,15 +435,18 @@
 
 
 def place_results(*refs):
-    sems = refs[-1]
-    half = len(refs) // 2
-    copies = [
-        pltpu.make_async_copy(refs[i], refs[half + i], sems.at[i]) for i in range(half)
-    ]
-    for copy in copies:
-        copy.start()
-    for copy in copies:
-        copy.wait()
+    count = (len(refs) - 2) // 3
+    given, placed, held = (refs[i * count : (i + 1) * count] for i in range(3))
+    load_s, store_s = refs[-2:]
+    loads = [pltpu.make_async_copy(given[i], held[i], load_s.at[i]) for i in range(count)]
+    stores = [pltpu.make_async_copy(held[i], placed[i], store_s.at[i]) for i in range(count)]
+    for load in loads:
+        load.start()
+    for load, store in zip(loads, stores):
+        load.wait()
+        store.start()
+    for store in stores:
+        store.wait()
 
 
 def per_device(
@@ -438,7 +472,18 @@
     pad = sel
     steps = np.arange(head // 2, dtype=np.float64) * (-2.0 * math.log(rope_base) / head)
     frequency = np.tile(np.exp(steps), 2).astype(np.float32)
-    gains = jnp.stack([query_gain, key_gain, jnp.asarray(frequency)])
+    arguments = (
+        positions,
+        router_logits,
+        queries[0],
+        keys[0],
+        values[0],
+        out_cotangent[0],
+        query_gain[None],
+        key_gain[None],
+        jnp.asarray(frequency)[None],
+    )
+    anywhere = pl.BlockSpec(memory_space=pl.ANY)
     vmem = pl.BlockSpec(memory_space=pltpu.VMEM)
     dma = pltpu.SemaphoreType.DMA
     n_g = 3 + n_seg * n_dp
@@ -453,9 +498,11 @@
             jax.ShapeDtypeStruct((1, head), F32),
             jax.ShapeDtypeStruct((1, head), F32),
         ),
-        in_specs=[vmem] * 7,
+        in_specs=[anywhere] * len(arguments),
         out_specs=(vmem,) * 7,
-        scratch_shapes=[
+        scratch_shapes=[pltpu.VMEM(a.shape, a.dtype) for a in arguments]
+        + [
+            dma((len(arguments),)),
             pltpu.VMEM((SEG_DEV, pad, 2 * head), BF16),
             pltpu.VMEM((SEG_DEV, pad, 2 * head), BF16),
             pltpu.VMEM((SEG_DEV - 1, cap, gw), BF16),
@@ -498,17 +545,18 @@
             dma((n_g,)),
         ],
         compiler_params=pltpu.CompilerParams(
-            collective_id=0, has_side_effects=True, vmem_limit_bytes=40 * 1024 * 1024
+            collective_id=0, has_side_effects=True, vmem_limit_bytes=56 * 1024 * 1024
         ),
-    )(positions, router_logits, queries[0], keys[0], values[0], out_cotangent[0], gains)
+    )(*arguments)
     count = len(results)
-    anywhere = pl.BlockSpec(memory_space=pl.ANY)
     out, gq, gk, gv, gl, gain_q, gain_k = pl.pallas_call(
         place_results,
         out_shape=tuple(jax.ShapeDtypeStruct(r.shape, r.dtype) for r in results),
         in_specs=[anywhere] * count,
         out_specs=(anywhere,) * count,
-        scratch_shapes=[dma((count,))],
+        scratch_shapes=[pltpu.VMEM(r.shape, r.dtype) for r in results]
+        + [dma((count,)), dma((count,))],
+        compiler_params=pltpu.CompilerParams(vmem_limit_bytes=56 * 1024 * 1024),
     )(*results)
     return (
         out[None],

time: 65.3 us -> 38 us (0.58)
  Pallas kernels: 56.2 us -> 37.2 us
  local copies, waits for them, and re-layouts: 8.06 us -> 0 us
    pallas_call x1, Pallas kernels: 22.1 us -> 1.92 us  [per_device(): pl.pallas_call(place_results, out_shape=tuple((jax.ShapeDtypeStruct(r.sha...]
    unnamed x32 -> x0, local copies, waits for them, and re-layouts: 8.06 us -> none
    pallas_call x1, Pallas kernels: 34.2 us -> 35.2 us  [per_device(): pl.pallas_call(functools.partial(kernel, n_seg, n_dp), out_shape=(jax.Sha...]
where the time goes in v3:
time: 38 us; the launch traced here: 37.8 us
  Pallas kernels  37.2 us (98%)
  between operations  0.64 us (2%)
    pallas_call x1, Pallas kernels, per_device(): pl.pallas_call(functools.partial(kernel, n_seg, n_dp), out_shape=(jax.Sha...  35.2 us
    pallas_call x1, Pallas kernels, per_device(): pl.pallas_call(place_results, out_shape=tuple((jax.ShapeDtypeStruct(r.sha...  1.92 us

profile of v3, /device:TPU:0, one launch (start us, length us, event | category | flops | bytes accessed | tf_op | source)
XLA Modules:
  0.0 37.8 jit_solution(16048840431934613789)
XLA Ops:
  0.6 35.2 %shard_map.144 = (bf16[48,3072]{1,0:T(8,128)(2,1)}, bf16[48,3072]{1,0:T(8,128)(2,1)}, bf16[48,512]{1,0:T(8,128)(2,1)}, bf16[48,512]{1,0:T(8,128)(2,1)}, f32[1,48...) custom-call(s32[1,48]{1,0:T(1,128)} %pos_hbm.1, f32[1,48]{1,0:T(1,128)} %logit_hbm.1, bf16[48,3072]{1,0:T(8,128)(2,1)} %bitcast.12, ...), custom_call_target="tpu_custom_call" | custom-call | tf_op jit(solution)/shard_map/pallas_call | solution.py:490
  35.9 1.9 %shard_map.145 = (bf16[48,3072]{1,0:T(8,128)(2,1)}, bf16[48,3072]{1,0:T(8,128)(2,1)}, bf16[48,512]{1,0:T(8,128)(2,1)}, bf16[48,512]{1,0:T(8,128)(2,1)}, f32[1,48...) custom-call(bf16[48,3072]{1,0:T(8,128)(2,1)} %get-tuple-element.21.refs_0_, ...), custom_call_target="tpu_custom_call" | custom-call | tf_op jit(solution)/shard_map/pallas_call | solution.py:552

commit v4 on v3

--- a/solution.py
+++ b/solution.py
@@ -40,6 +40,13 @@
     gq_in_hbm,
     gk_in_hbm,
     freq_hbm,
+    out_hbm,
+    gq_hbm,
+    gk_hbm,
+    gv_hbm,
+    gl_hbm,
+    gains_q_hbm,
+    gains_k_hbm,
     out_ref,
     gq_ref,
     gk_ref,
@@ -47,6 +54,7 @@
     gl_ref,
     gains_q_ref,
     gains_k_ref,
+    out_s,
     pos_ref,
     logit_ref,
     q_ref,
@@ -112,6 +120,16 @@
     loads = [pltpu.make_async_copy(a, b, in_s.at[i]) for i, (a, b) in enumerate(given)]
     for load in loads:
         load.start()
+    made = (
+        (out_ref, out_hbm),
+        (gl_ref, gl_hbm),
+        (gq_ref, gq_hbm),
+        (gk_ref, gk_hbm),
+        (gv_ref, gv_hbm),
+        (gains_q_ref, gains_q_hbm),
+        (gains_k_ref, gains_k_hbm),
+    )
+    saves = [pltpu.make_async_copy(a, b, out_s.at[i]) for i, (a, b) in enumerate(made)]
     cap, width_q = q_ref.shape
     width_k = k_ref.shape[1]
     head = freq_ref.shape[1]
@@ -339,6 +357,9 @@
     total_logit = (1.0 - gate[:, 0:1]) * jnp.sum(logit, axis=-1, keepdims=True)
     gl_ref[...] = jnp.sum(jnp.where(eye, total_logit, 0.0), axis=0, keepdims=True)
 
+    saves[0].start()
+    saves[1].start()
+
     def norm_back(grad, unit, inv, gain):
         turned = rot(grad.astype(F32), -1)
         term = jnp.sum(turned * unit, axis=0, keepdims=True)
@@ -381,6 +402,7 @@
         copy.wait_recv()
         term_q = query_back(o, term_q)
 
+    saves[2].start()
     for copy in kb_copies:
         copy.wait_recv()
     term_k = jnp.zeros((1, head), F32)
@@ -390,6 +412,9 @@
         gk_ref[:, cols] = grad
         gv_ref[:, cols] = rkb[t, :, head:]
         term_k = term_k + term
+
+    saves[3].start()
+    saves[4].start()
 
     which = lax.broadcasted_iota(jnp.int32, (8, head), 0)
     terms = jnp.where(which == 0, term_q, jnp.where(which == 1, term_k, 0.0))
@@ -429,6 +454,10 @@
     gains_q_ref[...] = terms[0:1] * over_q
     gains_k_ref[...] = terms[1:2] * over_k
 
+    saves[5].start()
+    saves[6].start()
+    for save in saves:
+        save.wait()
     mine = kv_copies + q_copies + d_copies + z_copies + dz_copies
     for copy in mine + b_copies + e_copies + kb_copies + last:
         copy.wait_send()
@@ -484,12 +513,9 @@
         jnp.asarray(frequency)[None],
     )
     anywhere = pl.BlockSpec(memory_space=pl.ANY)
-    vmem = pl.BlockSpec(memory_space=pltpu.VMEM)
     dma = pltpu.SemaphoreType.DMA
     n_g = 3 + n_seg * n_dp
-    results = pl.pallas_call(
-        functools.partial(kernel, n_seg, n_dp),
-        out_shape=(
+    made = (
             jax.ShapeDtypeStruct((cap, width_q), BF16),
             jax.ShapeDtypeStruct((cap, width_q), BF16),
             jax.ShapeDtypeStruct((cap, width_k), BF16),
@@ -497,10 +523,15 @@
             jax.ShapeDtypeStruct((1, cap), F32),
             jax.ShapeDtypeStruct((1, head), F32),
             jax.ShapeDtypeStruct((1, head), F32),
-        ),
+        )
+    results = pl.pallas_call(
+        functools.partial(kernel, n_seg, n_dp),
+        out_shape=made,
         in_specs=[anywhere] * len(arguments),
-        out_specs=(vmem,) * 7,
-        scratch_shapes=[pltpu.VMEM(a.shape, a.dtype) for a in arguments]
+        out_specs=(anywhere,) * len(made),
+        scratch_shapes=[pltpu.VMEM(a.shape, a.dtype) for a in made]
+        + [dma((len(made),))]
+        + [pltpu.VMEM(a.shape, a.dtype) for a in arguments]
         + [
             dma((len(arguments),)),
             pltpu.VMEM((SEG_DEV, pad, 2 * head), BF16),

time: 38 us -> 37.8 us (level)
  no operation moved by 1% of the time
where the time goes in v4:
time: 37.8 us; the launch traced here: 37.6 us
  Pallas kernels  37 us (98%)
  between operations  0.64 us (2%)
    pallas_call x1, Pallas kernels, per_device(): pl.pallas_call(functools.partial(kernel, n_seg, n_dp), out_shape=made, in...  35 us
    pallas_call x1, Pallas kernels, per_device(): pl.pallas_call(place_results, out_shape=tuple((jax.ShapeDtypeStruct(r.sha...  1.92 us

profile of v4, /device:TPU:0, one launch (start us, length us, event | category | flops | bytes accessed | tf_op | source)
XLA Modules:
  0.0 37.6 jit_solution(3786070553666126209)
XLA Ops:
  0.6 35.0 %shard_map.144 = (bf16[48,3072]{1,0:T(8,128)(2,1)}, bf16[48,3072]{1,0:T(8,128)(2,1)}, bf16[48,512]{1,0:T(8,128)(2,1)}, bf16[48,512]{1,0:T(8,128)(2,1)}, f32[1,48...) custom-call(s32[1,48]{1,0:T(1,128)} %pos_hbm.1, f32[1,48]{1,0:T(1,128)} %logit_hbm.1, bf16[48,3072]{1,0:T(8,128)(2,1)} %bitcast.12, ...), custom_call_target="tpu_custom_call" | custom-call | tf_op jit(solution)/shard_map/pallas_call | solution.py:527
  35.7 1.9 %shard_map.145 = (bf16[48,3072]{1,0:T(8,128)(2,1)}, bf16[48,3072]{1,0:T(8,128)(2,1)}, bf16[48,512]{1,0:T(8,128)(2,1)}, bf16[48,512]{1,0:T(8,128)(2,1)}, f32[1,48...) custom-call(bf16[48,3072]{1,0:T(8,128)(2,1)} %get-tuple-element.21.refs_0_, ...), custom_call_target="tpu_custom_call" | custom-call | tf_op jit(solution)/shard_map/pallas_call | solution.py:583

commit v5 on v4

--- a/solution.py
+++ b/solution.py
@@ -78,6 +78,7 @@
     kinv,
     kv_all,
     dkv_p,
+    dkv_h,
     dkv_r,
     satt,
     ratt,
@@ -327,12 +328,13 @@
     dscore = (probs * (dprob - delta)).astype(BF16)
     dkv_p[:, :, 0:head] = (dot(dscore, q_rows, TN) * scale).reshape(n_seg, sel, head)
     dkv_p[:, :, head:] = dot(probs_b, d_rows, TN).reshape(n_seg, sel, head)
+    dkv_h[...] = dkv_p[...].astype(BF16)
     dz_copies = []
     for o in far:
-        copy = remote(dkv_p.at[far[o]], dkv_r.at[seg], dz_s.at[o], dz_r.at[o], ctx=far_dev[o])
+        copy = remote(dkv_h.at[far[o]], dkv_r.at[seg], dz_s.at[o], dz_r.at[o], ctx=far_dev[o])
         copy.start()
         dz_copies.append(copy)
-    dkv_r[seg] = dkv_p[seg]
+    dkv_r[seg] = jnp.zeros((sel, 2 * head), BF16)
 
     dq = (dot(dscore, keys, NN) * scale).astype(BF16)
     sdq[...] = dot(pick, heads_across(dq), TN).astype(BF16).reshape(SEG_DEV, pad, gw)
@@ -385,9 +387,9 @@
 
     for copy in dz_copies:
         copy.wait_recv()
-    dkv = dkv_r[0]
-    for s in range(1, n_seg):
-        dkv = dkv + dkv_r[s]
+    dkv = dkv_p[seg]
+    for s in range(n_seg):
+        dkv = dkv + dkv_r[s].astype(F32)
     skb[...] = dot(pick, dkv.astype(BF16), TN).astype(BF16).reshape(SEG_DEV, pad, 2 * head)
     kb_copies = []
     for o in order:
@@ -547,7 +549,8 @@
             pltpu.VMEM((heads_k, cap, head), F32),
             pltpu.VMEM((n_seg, sel, 2 * head), BF16),
             pltpu.VMEM((n_seg, sel, 2 * head), F32),
-            pltpu.VMEM((n_seg, sel, 2 * head), F32),
+            pltpu.VMEM((n_seg, sel, 2 * head), BF16),
+            pltpu.VMEM((n_seg, sel, 2 * head), BF16),
             pltpu.VMEM((SEG_DEV, pad, gw), BF16),
             pltpu.VMEM((SEG_DEV, cap, gw), BF16),
             pltpu.VMEM((SEG_DEV, pad, gw), BF16),

time: 37.8 us -> 36 us (0.952)
  Pallas kernels: 37 us -> 35.2 us
    pallas_call x1, Pallas kernels: 35 us -> 33.3 us  [per_device(): pl.pallas_call(functools.partial(kernel, n_seg, n_dp), out_shape=made, in...]
where the time goes in v5:
time: 36 us; the launch traced here: 35.9 us
  Pallas kernels  35.2 us (98%)
  between operations  0.64 us (2%)
    pallas_call x1, Pallas kernels, per_device(): pl.pallas_call(functools.partial(kernel, n_seg, n_dp), out_shape=made, in...  33.3 us
    pallas_call x1, Pallas kernels, per_device(): pl.pallas_call(place_results, out_shape=tuple((jax.ShapeDtypeStruct(r.sha...  1.92 us

profile of v5, /device:TPU:0, one launch (start us, length us, event | category | flops | bytes accessed | tf_op | source)
XLA Modules:
  0.0 35.9 jit_solution(15051107414036607701)
XLA Ops:
  0.6 33.3 %shard_map.144 = (bf16[48,3072]{1,0:T(8,128)(2,1)}, bf16[48,3072]{1,0:T(8,128)(2,1)}, bf16[48,512]{1,0:T(8,128)(2,1)}, bf16[48,512]{1,0:T(8,128)(2,1)}, f32[1,48...) custom-call(s32[1,48]{1,0:T(1,128)} %pos_hbm.1, f32[1,48]{1,0:T(1,128)} %logit_hbm.1, bf16[48,3072]{1,0:T(8,128)(2,1)} %bitcast.12, ...), custom_call_target="tpu_custom_call" | custom-call | tf_op jit(solution)/shard_map/pallas_call | solution.py:529
  34.0 1.9 %shard_map.145 = (bf16[48,3072]{1,0:T(8,128)(2,1)}, bf16[48,3072]{1,0:T(8,128)(2,1)}, bf16[48,512]{1,0:T(8,128)(2,1)}, bf16[48,512]{1,0:T(8,128)(2,1)}, f32[1,48...) custom-call(bf16[48,3072]{1,0:T(8,128)(2,1)} %get-tuple-element.21.refs_0_, ...), custom_call_target="tpu_custom_call" | custom-call | tf_op jit(solution)/shard_map/pallas_call | solution.py:586
